TPU v7x, 1024 devices: a whole 4x4x32 slice. The times are simulated.
1024 devices in a mesh: seq: 128 (over z, y), head: 8 (over x, core).
Axes of the slice: x: 4, y: 4, z: 32, core: 2. Of those that a mesh axis runs over, the one named last changes fastest.
Arguments:
- queries: bfloat16 [16384, 4096], P('seq', 'head'), may hold values from -40 to 40
- keys_in: bfloat16 [16384, 1024], P('seq', 'head'), may hold values from -4 to 4
- values_in: bfloat16 [16384, 1024], P('seq', 'head'), may hold values from -20 to 20
- norm_gain: float32 [4096], P('head'), may hold values from 0.1 to 1.9
- grad_out: bfloat16 [16384, 4096], P('seq', 'head'), may hold values from -6 to 6
- nearby_block_mask: int32 [128, 16], P('seq'), may hold values from 0 to 1, as said below
Outputs:
- normed_out: bfloat16 [16384, 4096], P('seq', 'head')
- grad_queries: bfloat16 [16384, 4096], P('seq', 'head')
- grad_keys: bfloat16 [16384, 1024], P('seq', 'head')
- grad_values: bfloat16 [16384, 1024], P('seq', 'head')
Inputs may be any that keep to these rules, and one draw needn't show every extreme that they name: nearby_block_mask[b, j] is 0 wherever key block (b - 8) + j lies outside the scene, and 1 where that block is b itself.
All inputs are finite; a program needn't handle non-finite values.
Results may differ from a plain program's by a relative error of at most 0.013.
Values may be sent and summed in bfloat16 or wider, within the bound.
No kernel may reach another device: no remote copies, remote signals or barrier semaphores. Data moves between devices by JAX's collectives and lax.ppermute only.
A program may use at most 32 MiB of HBM per device.

v0:
```python
from functools import partial

import jax
import jax.numpy as jnp
from jax import lax
from jax.sharding import PartitionSpec as P

HEADS = 32
KV_HEADS = 8
DH = 128
BLK = 128


NEGATIVE = -1e30
EPSILON = 1e-06


def shifted(array, axis, by):
    length = lax.axis_size(axis)
    pairs = [(i, i + by) for i in range(length) if 0 <= i + by < length]
    return lax.ppermute(array, axis, pairs)


def per_device(queries, keys_in, values_in, norm_gain, grad_out, nearby_block_mask):
    rows_dev = queries.shape[0]
    kv_dev = keys_in.shape[1] // DH
    group_size = HEADS // KV_HEADS
    blocks_dev = rows_dev // BLK
    span_devices = min(16, lax.axis_size("seq"))
    half_span = span_devices // 2
    scaling = DH ** (-0.5)
    features = HEADS * DH
    q_dev = queries.reshape(rows_dev, kv_dev, group_size, DH)
    offsets = [0] + [slot - half_span for slot in range(span_devices) if slot != half_span]

    def blocks_at(offset):
        start = (offset + half_span) * blocks_dev
        return nearby_block_mask[:, start : start + blocks_dev]

    def score_block(k_far, blocks):
        raw = jnp.einsum(
            "qcge,tce->cgqt",
            q_dev,
            k_far.reshape(rows_dev, kv_dev, DH),
            preferred_element_type=jnp.float32,
        )
        widened = jnp.repeat(jnp.repeat(blocks, BLK, axis=0), BLK, axis=1) > 0
        return jnp.where(widened[None, None], raw * scaling, NEGATIVE)

    def absorb(carried, k_far, v_far, blocks):
        row_top, row_total, numerator = carried
        scores = score_block(k_far, blocks)
        new_top = jnp.maximum(row_top, scores.max(axis=-1))
        rescale = jnp.exp(row_top - new_top)
        weights = jnp.exp(scores - new_top[..., None])
        part_sum = jnp.einsum(
            "cgqt,tce->qcge",
            weights.astype(jnp.bfloat16),
            v_far.reshape(rows_dev, kv_dev, DH),
            preferred_element_type=jnp.float32,
        )
        numerator = numerator * jnp.transpose(rescale, (2, 0, 1))[..., None] + part_sum
        return (new_top, row_total * rescale + weights.sum(axis=-1), numerator)

    carried = (
        jnp.full((kv_dev, group_size, rows_dev), NEGATIVE, jnp.float32),
        jnp.zeros((kv_dev, group_size, rows_dev), jnp.float32),
        jnp.zeros((rows_dev, kv_dev, group_size, DH), jnp.float32),
    )
    kept_pairs = []
    for offset in offsets:
        blocks = blocks_at(offset)
        if offset == 0:
            k_far, v_far = (keys_in, values_in)
        else:
            k_far, v_far = shifted((keys_in, values_in), "seq", -offset)
        kept_pairs.append((k_far, v_far))
        carried = lax.cond(
            jnp.any(blocks > 0),
            partial(absorb, k_far=k_far, v_far=v_far, blocks=blocks),
            lambda same: same,
            carried,
        )
    row_top, row_total, numerator = carried
    attended = numerator / jnp.transpose(row_total, (2, 0, 1))[..., None]
    log_total = row_top + jnp.log(row_total)
    flat = attended.reshape(rows_dev, -1)
    upstream = grad_out.astype(jnp.float32) * norm_gain
    square_sum = lax.psum(jnp.sum(flat * flat, axis=-1), "head")
    root = jnp.sqrt(square_sum / features + EPSILON)
    normed = flat / root[:, None]
    inner = lax.psum(jnp.sum(upstream * normed, axis=-1), "head")
    normed_out = (norm_gain * normed).astype(jnp.bfloat16)
    d_attended = ((upstream - normed * (inner / features)[:, None]) / root[:, None]).astype(
        jnp.bfloat16
    )
    do_dev = d_attended.reshape(rows_dev, kv_dev, group_size, DH)
    delta = jnp.transpose(jnp.sum(do_dev.astype(jnp.float32) * attended, axis=-1), (1, 2, 0))

    def pair_terms(k_far, v_far, blocks):
        k_dev = k_far.reshape(rows_dev, kv_dev, DH)
        v_dev = v_far.reshape(rows_dev, kv_dev, DH)
        scores = score_block(k_far, blocks)
        prob = jnp.exp(scores - log_total[..., None])
        d_prob = jnp.einsum("qcge,tce->cgqt", do_dev, v_dev, preferred_element_type=jnp.float32)
        d_score = (prob * (d_prob - delta[..., None])).astype(jnp.bfloat16)
        grad_q = (
            jnp.einsum("cgqt,tce->qcge", d_score, k_dev, preferred_element_type=jnp.float32)
            * scaling
        ).astype(jnp.bfloat16)
        grad_k = (
            jnp.einsum("cgqt,qcge->tce", d_score, q_dev, preferred_element_type=jnp.float32)
            * scaling
        ).astype(jnp.bfloat16)
        grad_v = jnp.einsum(
            "cgqt,qcge->tce", prob.astype(jnp.bfloat16), do_dev, preferred_element_type=jnp.float32
        ).astype(jnp.bfloat16)
        return (grad_q, grad_k.reshape(rows_dev, -1), grad_v.reshape(rows_dev, -1))

    zero_terms = (
        jnp.zeros((rows_dev, kv_dev, group_size, DH), jnp.bfloat16),
        jnp.zeros(keys_in.shape, jnp.bfloat16),
        jnp.zeros(keys_in.shape, jnp.bfloat16),
    )
    grad_q_sum = jnp.zeros((rows_dev, kv_dev, group_size, DH), jnp.float32)
    grad_k_sum = jnp.zeros(keys_in.shape, jnp.float32)
    grad_v_sum = jnp.zeros(keys_in.shape, jnp.float32)
    for position, offset in enumerate(offsets):
        blocks = blocks_at(offset)
        if offset == 0:
            k_far, v_far = (keys_in, values_in)
        else:
            k_far, v_far = shifted((keys_in, values_in), "seq", -offset)
        terms = lax.cond(
            jnp.any(blocks > 0),
            partial(pair_terms, k_far, v_far),
            lambda unused: zero_terms,
            blocks,
        )
        grad_q_sum = grad_q_sum + terms[0].astype(jnp.float32)
        if offset == 0:
            returned = (terms[1], terms[2])
        else:
            returned = shifted((terms[1], terms[2]), "seq", offset)
        grad_k_sum = grad_k_sum + returned[0].astype(jnp.float32)
        grad_v_sum = grad_v_sum + returned[1].astype(jnp.float32)
    grad_queries = grad_q_sum.reshape(rows_dev, -1).astype(jnp.bfloat16)
    return (
        normed_out,
        grad_queries,
        grad_k_sum.astype(jnp.bfloat16),
        grad_v_sum.astype(jnp.bfloat16),
    )


def solution(mesh):
    in_specs = (
        P("seq", "head"),
        P("seq", "head"),
        P("seq", "head"),
        P("head"),
        P("seq", "head"),
        P("seq", None),
    )
    out_specs = (P("seq", "head"), P("seq", "head"), P("seq", "head"), P("seq", "head"))
    return jax.shard_map(
        per_device, mesh=mesh, in_specs=in_specs, out_specs=out_specs, check_vma=False
    )
```

profile of v0, /device:TPU:256, one launch (start us, length us, event | category | flops | bytes accessed | tf_op | source)
XLA Modules:
  0.0 369.4 jit_solution(1967664194166955020)
XLA Ops:
  0.6 4.0 %collective-permute-start.24 = (bf16[128,128]{1,0:T(8,128)(2,1)}, bf16[128,128]{1,0:T(8,128)(2,1)S(1)}, u32[]{:S(2)}, u32[]{:S(2)}) collective-permute-start(bf16[128,128]{1,0:T(8,128)(2,1)} %param.71), channel_id=1, source_target_pairs={{40,0},{48,8},{56,16},{64,24},{72,32},{80,40},{88,48},{96,56},{104... | collective-permute-start | bytes 98312 | tf_op jit(solution)/shard_map/ppermute | solution.py:21
  22.0 5.9 %collective-permute-start.10 = (bf16[128,128]{1,0:T(8,128)(2,1)}, bf16[128,128]{1,0:T(8,128)(2,1)S(1)}, u32[]{:S(2)}, u32[]{:S(2)}) collective-permute-start(bf16[128,128]{1,0:T(8,128)(2,1)} %param.71), channel_id=1, source_target_pairs={{0,24},{8,32},{16,40},{24,48},{32,56},{40,64},{48,72},{56,80},{64,... | collective-permute-start | bytes 98312 | tf_op jit(solution)/shard_map/ppermute | solution.py:21
  34.5 7.4 %collective-permute-start.4 = (bf16[128,128]{1,0:T(8,128)(2,1)}, bf16[128,128]{1,0:T(8,128)(2,1)S(1)}, u32[]{:S(2)}, u32[]{:S(2)}) collective-permute-start(bf16[128,128]{1,0:T(8,128)(2,1)} %param.71), channel_id=1, source_target_pairs={{0,48},{8,56},{16,64},{24,72},{32,80},{40,88},{48,96},{56,104},{64... | collective-permute-start | bytes 98312 | tf_op jit(solution)/shard_map/ppermute | solution.py:21
  41.9 6.9 %collective-permute-start.2 = (bf16[128,128]{1,0:T(8,128)(2,1)}, bf16[128,128]{1,0:T(8,128)(2,1)S(1)}, u32[]{:S(2)}, u32[]{:S(2)}) collective-permute-start(bf16[128,128]{1,0:T(8,128)(2,1)} %param.71), channel_id=1, source_target_pairs={{0,56},{8,64},{16,72},{24,80},{32,88},{40,96},{48,104},{56,112},{6... | collective-permute-start | bytes 98312 | tf_op jit(solution)/shard_map/ppermute | solution.py:21
  48.8 6.4 %collective-permute-start = (bf16[128,128]{1,0:T(8,128)(2,1)}, bf16[128,128]{1,0:T(8,128)(2,1)S(1)}, u32[]{:S(2)}, u32[]{:S(2)}) collective-permute-start(bf16[128,128]{1,0:T(8,128)(2,1)} %param.71), channel_id=1, source_target_pairs={{0,64},{8,72},{16,80},{24,88},{32,96},{40,104},{48,112},{56,120},{... | collective-permute-start | bytes 98312 | tf_op jit(solution)/shard_map/ppermute | solution.py:21
  60.4 4.2 %collective-permute-start.19 = (bf16[128,128]{1,0:T(8,128)(2,1)}, bf16[128,128]{1,0:T(8,128)(2,1)S(1)}, u32[]{:S(2)}, u32[]{:S(2)}) collective-permute-start(bf16[128,128]{1,0:T(8,128)(2,1)} %param.72), channel_id=1, source_target_pairs={{16,0},{24,8},{32,16},{40,24},{48,32},{56,40},{64,48},{72,56},{80,... | collective-permute-start | bytes 98312 | tf_op jit(solution)/shard_map/ppermute | solution.py:21
  74.6 5.2 %collective-permute-start.11 = (bf16[128,128]{1,0:T(8,128)(2,1)}, bf16[128,128]{1,0:T(8,128)(2,1)S(1)}, u32[]{:S(2)}, u32[]{:S(2)}) collective-permute-start(bf16[128,128]{1,0:T(8,128)(2,1)} %param.72), channel_id=1, source_target_pairs={{0,24},{8,32},{16,40},{24,48},{32,56},{40,64},{48,72},{56,80},{64,... | collective-permute-start | bytes 98312 | tf_op jit(solution)/shard_map/ppermute | solution.py:21
  86.1 8.4 %collective-permute-start.5 = (bf16[128,128]{1,0:T(8,128)(2,1)}, bf16[128,128]{1,0:T(8,128)(2,1)S(1)}, u32[]{:S(2)}, u32[]{:S(2)}) collective-permute-start(bf16[128,128]{1,0:T(8,128)(2,1)} %param.72), channel_id=1, source_target_pairs={{0,48},{8,56},{16,64},{24,72},{32,80},{40,88},{48,96},{56,104},{64... | collective-permute-start | bytes 98312 | tf_op jit(solution)/shard_map/ppermute | solution.py:21
  94.5 6.0 %collective-permute-start.3 = (bf16[128,128]{1,0:T(8,128)(2,1)}, bf16[128,128]{1,0:T(8,128)(2,1)S(1)}, u32[]{:S(2)}, u32[]{:S(2)}) collective-permute-start(bf16[128,128]{1,0:T(8,128)(2,1)} %param.72), channel_id=1, source_target_pairs={{0,56},{8,64},{16,72},{24,80},{32,88},{40,96},{48,104},{56,112},{6... | collective-permute-start | bytes 98312 | tf_op jit(solution)/shard_map/ppermute | solution.py:21
  100.5 4.4 %collective-permute-start.1 = (bf16[128,128]{1,0:T(8,128)(2,1)}, bf16[128,128]{1,0:T(8,128)(2,1)S(1)}, u32[]{:S(2)}, u32[]{:S(2)}) collective-permute-start(bf16[128,128]{1,0:T(8,128)(2,1)} %param.72), channel_id=1, source_target_pairs={{0,64},{8,72},{16,80},{24,88},{32,96},{40,104},{48,112},{56,120},{... | collective-permute-start | bytes 98312 | tf_op jit(solution)/shard_map/ppermute | solution.py:21
  111.1 5.7 %collective-permute-start.27 = (bf16[128,128]{1,0:T(8,128)(2,1)}, bf16[128,128]{1,0:T(8,128)(2,1)}, u32[]{:S(2)}, u32[]{:S(2)}) collective-permute-start(bf16[128,128]{1,0:T(8,128)(2,1)} %param.72), channel_id=1, source_target_pairs={{48,0},{56,8},{64,16},{72,24},{80,32},{88,40},{96,48},{104,56},{11... | collective-permute-start | bytes 98312 | tf_op jit(solution)/shard_map/ppermute | solution.py:21
  165.4 4.6 %conditional.45 = (f32[1,4,128]{2,1,0:T(4,128)}, f32[1,4,128]{2,1,0:T(4,128)S(1)}, f32[128,1,4,128]{3,0,2,1:T(8,128)S(1)}) conditional(s32[]{:T(128)} %bitcast.529, (f32[1,4,128]{2,1,0:T(4,128)}, f32[1,4,128]{2,1,0:T(4,128)S(1)}, f32[128,1,4,128]{3,0,2,1:T(8,128)S(1)}) %get-tuple-element.1625, (s32[1,1]{1,0:T(1,128)}, ...), branch_computations={%region_52.53_spmd, %region_53.56_spmd} | conditional | flops 34145792 | bytes 1536034 | solution.py:78
  171.1 12.4 %psum.14 = f32[128]{0:T(128)S(1)} all-reduce(f32[128]{0:T(128)S(1)} %get-tuple-element.1370), channel_id=1, replica_groups=mesh['seq'=128,'head'=8] {'head'}, use_global_device_ids=true, to_apply=%region_65.66 | all-reduce | flops 128 | bytes 1024 | tf_op jit(solution)/shard_map/psum | solution.py:89
  184.6 12.4 %psum.15 = f32[128]{0:T(128)S(1)} all-reduce(f32[128]{0:T(128)S(1)} %multiply_reduce_fusion.1), channel_id=1, replica_groups=mesh['seq'=128,'head'=8] {'head'}, use_global_device_ids=true, to_apply=%region_67.68 | all-reduce | flops 128 | bytes 1024 | tf_op jit(solution)/shard_map/psum | solution.py:92
  199.7 19.8 %collective-permute-start.30 = (bf16[128,128]{1,0:T(8,128)(2,1)S(1)}, bf16[128,128]{1,0:T(8,128)(2,1)S(1)}, u32[]{:S(2)}, u32[]{:S(2)}) collective-permute-start(bf16[128,128]{1,0:T(8,128)(2,1)S(1)} %get-tuple-element.950), channel_id=1, source_target_pairs={{64,0},{72,8},{80,16},{88,24},{96,32},{104,40},{112,48},{120,56},{... | collective-permute-start | bytes 98312 | tf_op jit(solution)/shard_map/ppermute | solution.py:21
  251.8 8.7 %collective-permute-start.36 = (bf16[128,128]{1,0:T(8,128)(2,1)S(1)}, bf16[128,128]{1,0:T(8,128)(2,1)S(1)}, u32[]{:S(2)}, u32[]{:S(2)}) collective-permute-start(bf16[128,128]{1,0:T(8,128)(2,1)S(1)} %get-tuple-element.956), channel_id=1, source_target_pairs={{16,0},{24,8},{32,16},{40,24},{48,32},{56,40},{64,48},{72,56},{80,... | collective-permute-start | bytes 98312 | tf_op jit(solution)/shard_map/ppermute | solution.py:21
  278.0 5.8 %collective-permute-start.39 = (bf16[128,128]{1,0:T(8,128)(2,1)}, bf16[128,128]{1,0:T(8,128)(2,1)}, u32[]{:S(2)}, u32[]{:S(2)}) collective-permute-start(bf16[128,128]{1,0:T(8,128)(2,1)} %get-tuple-element.959), channel_id=1, source_target_pairs={{0,16},{8,24},{16,32},{24,40},{32,48},{40,56},{48,64},{56,72},{64,... | collective-permute-start | bytes 98312 | tf_op jit(solution)/shard_map/ppermute | solution.py:21
  306.9 11.2 %collective-permute-start.57 = (bf16[128,128]{1,0:T(8,128)(2,1)}, bf16[128,128]{1,0:T(8,128)(2,1)S(1)}, u32[]{:S(2)}, u32[]{:S(2)}) collective-permute-start(bf16[128,128]{1,0:T(8,128)(2,1)} %copy-done.51), channel_id=1, source_target_pairs={{0,40},{8,48},{16,56},{24,64},{32,72},{40,80},{48,88},{56,96},{64,... | collective-permute-start | bytes 98312 | tf_op jit(solution)/shard_map/ppermute | solution.py:21
  318.1 9.0 %collective-permute-start.58 = (bf16[128,128]{1,0:T(8,128)(2,1)}, bf16[128,128]{1,0:T(8,128)(2,1)S(1)}, u32[]{:S(2)}, u32[]{:S(2)}) collective-permute-start(bf16[128,128]{1,0:T(8,128)(2,1)} %copy-done.54), channel_id=1, source_target_pairs={{0,48},{8,56},{16,64},{24,72},{32,80},{40,88},{48,96},{56,104},{64... | collective-permute-start | bytes 98312 | tf_op jit(solution)/shard_map/ppermute | solution.py:21
  327.2 5.4 %collective-permute-start.59 = (bf16[128,128]{1,0:T(8,128)(2,1)}, bf16[128,128]{1,0:T(8,128)(2,1)S(1)}, u32[]{:S(2)}, u32[]{:S(2)}) collective-permute-start(bf16[128,128]{1,0:T(8,128)(2,1)} %copy-done.57), channel_id=1, source_target_pairs={{0,56},{8,64},{16,72},{24,80},{32,88},{40,96},{48,104},{56,112},{6... | collective-permute-start | bytes 98312 | tf_op jit(solution)/shard_map/ppermute | solution.py:21
  336.9 5.0 %collective-permute-start.41 = (bf16[128,128]{1,0:T(8,128)(2,1)S(1)}, bf16[128,128]{1,0:T(8,128)(2,1)S(1)}, u32[]{:S(2)}, u32[]{:S(2)}) collective-permute-start(bf16[128,128]{1,0:T(8,128)(2,1)S(1)} %copy-done.50), channel_id=1, source_target_pairs={{0,32},{8,40},{16,48},{24,56},{32,64},{40,72},{48,80},{56,88},{64,... | collective-permute-start | bytes 98312 | tf_op jit(solution)/shard_map/ppermute | solution.py:21
  341.9 6.4 %collective-permute-start.42 = (bf16[128,128]{1,0:T(8,128)(2,1)S(1)}, bf16[128,128]{1,0:T(8,128)(2,1)S(1)}, u32[]{:S(2)}, u32[]{:S(2)}) collective-permute-start(bf16[128,128]{1,0:T(8,128)(2,1)S(1)} %copy-done.53), channel_id=1, source_target_pairs={{0,40},{8,48},{16,56},{24,64},{32,72},{40,80},{48,88},{56,96},{64,... | collective-permute-start | bytes 98312 | tf_op jit(solution)/shard_map/ppermute | solution.py:21
  348.3 10.7 %collective-permute-start.43 = (bf16[128,128]{1,0:T(8,128)(2,1)S(1)}, bf16[128,128]{1,0:T(8,128)(2,1)S(1)}, u32[]{:S(2)}, u32[]{:S(2)}) collective-permute-start(bf16[128,128]{1,0:T(8,128)(2,1)S(1)} %copy-done.56), channel_id=1, source_target_pairs={{0,48},{8,56},{16,64},{24,72},{32,80},{40,88},{48,96},{56,104},{64... | collective-permute-start | bytes 98312 | tf_op jit(solution)/shard_map/ppermute | solution.py:21
  363.3 4.6 %collective-permute-done.44 = bf16[128,128]{1,0:T(8,128)(2,1)S(1)} collective-permute-done((bf16[128,128]{1,0:T(8,128)(2,1)S(1)}, bf16[128,128]{1,0:T(8,128)(2,1)S(1)}, u32[]{:S(2)}, u32[]{:S(2)}) %collective-permute-start.44) | collective-permute-done | bytes 32800 | tf_op jit(solution)/shard_map/ppermute | solution.py:21
  (403 shorter events, 220.5 us)
Async XLA Ops:
  22.0 26.8 %collective-permute-start.10 = (bf16[128,128]{1,0:T(8,128)(2,1)}, bf16[128,128]{1,0:T(8,128)(2,1)S(1)}, u32[]{:S(2)}, u32[]{:S(2)}) collective-permute-start(bf16[128,128]{1,0:T(8,128)(2,1)} %param.71), channel_id=1, source_target_pairs={{0,24},{8,32},{16,40},{24,48},{32,56},{40,64},{48,72},{56,80},{64,... | collective-permute-start | bytes 98312 | tf_op jit(solution)/shard_map/ppermute | solution.py:21
  27.9 27.3 %collective-permute-start.8 = (bf16[128,128]{1,0:T(8,128)(2,1)}, bf16[128,128]{1,0:T(8,128)(2,1)S(1)}, u32[]{:S(2)}, u32[]{:S(2)}) collective-permute-start(bf16[128,128]{1,0:T(8,128)(2,1)} %param.71), channel_id=1, source_target_pairs={{0,32},{8,40},{16,48},{24,56},{32,64},{40,72},{48,80},{56,88},{64,... | collective-permute-start | bytes 98312 | tf_op jit(solution)/shard_map/ppermute | solution.py:21
  31.8 26.7 %collective-permute-start.6 = (bf16[128,128]{1,0:T(8,128)(2,1)}, bf16[128,128]{1,0:T(8,128)(2,1)S(1)}, u32[]{:S(2)}, u32[]{:S(2)}) collective-permute-start(bf16[128,128]{1,0:T(8,128)(2,1)} %param.71), channel_id=1, source_target_pairs={{0,40},{8,48},{16,56},{24,64},{32,72},{40,80},{48,88},{56,96},{64,... | collective-permute-start | bytes 98312 | tf_op jit(solution)/shard_map/ppermute | solution.py:21
  34.5 25.9 %collective-permute-start.4 = (bf16[128,128]{1,0:T(8,128)(2,1)}, bf16[128,128]{1,0:T(8,128)(2,1)S(1)}, u32[]{:S(2)}, u32[]{:S(2)}) collective-permute-start(bf16[128,128]{1,0:T(8,128)(2,1)} %param.71), channel_id=1, source_target_pairs={{0,48},{8,56},{16,64},{24,72},{32,80},{40,88},{48,96},{56,104},{64... | collective-permute-start | bytes 98312 | tf_op jit(solution)/shard_map/ppermute | solution.py:21
  74.6 25.9 %collective-permute-start.11 = (bf16[128,128]{1,0:T(8,128)(2,1)}, bf16[128,128]{1,0:T(8,128)(2,1)S(1)}, u32[]{:S(2)}, u32[]{:S(2)}) collective-permute-start(bf16[128,128]{1,0:T(8,128)(2,1)} %param.72), channel_id=1, source_target_pairs={{0,24},{8,32},{16,40},{24,48},{32,56},{40,64},{48,72},{56,80},{64,... | collective-permute-start | bytes 98312 | tf_op jit(solution)/shard_map/ppermute | solution.py:21
  83.1 25.4 %collective-permute-start.7 = (bf16[128,128]{1,0:T(8,128)(2,1)}, bf16[128,128]{1,0:T(8,128)(2,1)S(1)}, u32[]{:S(2)}, u32[]{:S(2)}) collective-permute-start(bf16[128,128]{1,0:T(8,128)(2,1)} %param.72), channel_id=1, source_target_pairs={{0,40},{8,48},{16,56},{24,64},{32,72},{40,80},{48,88},{56,96},{64,... | collective-permute-start | bytes 98312 | tf_op jit(solution)/shard_map/ppermute | solution.py:21
  104.9 65.1 %collective-permute-start.26 = (bf16[128,128]{1,0:T(8,128)(2,1)}, bf16[128,128]{1,0:T(8,128)(2,1)}, u32[]{:S(2)}, u32[]{:S(2)}) collective-permute-start(bf16[128,128]{1,0:T(8,128)(2,1)} %param.71), channel_id=1, source_target_pairs={{48,0},{56,8},{64,16},{72,24},{80,32},{88,40},{96,48},{104,56},{11... | collective-permute-start | bytes 98312 | tf_op jit(solution)/shard_map/ppermute | solution.py:21
  108.6 61.5 %collective-permute-start.28 = (bf16[128,128]{1,0:T(8,128)(2,1)}, bf16[128,128]{1,0:T(8,128)(2,1)S(1)}, u32[]{:S(2)}, u32[]{:S(2)}) collective-permute-start(bf16[128,128]{1,0:T(8,128)(2,1)} %param.71), channel_id=1, source_target_pairs={{56,0},{64,8},{72,16},{80,24},{88,32},{96,40},{104,48},{112,56},{1... | collective-permute-start | bytes 98312 | tf_op jit(solution)/shard_map/ppermute | solution.py:21
  111.1 59.0 %collective-permute-start.27 = (bf16[128,128]{1,0:T(8,128)(2,1)}, bf16[128,128]{1,0:T(8,128)(2,1)}, u32[]{:S(2)}, u32[]{:S(2)}) collective-permute-start(bf16[128,128]{1,0:T(8,128)(2,1)} %param.72), channel_id=1, source_target_pairs={{48,0},{56,8},{64,16},{72,24},{80,32},{88,40},{96,48},{104,56},{11... | collective-permute-start | bytes 98312 | tf_op jit(solution)/shard_map/ppermute | solution.py:21
  116.8 48.6 %collective-permute-start.25 = (bf16[128,128]{1,0:T(8,128)(2,1)}, bf16[128,128]{1,0:T(8,128)(2,1)}, u32[]{:S(2)}, u32[]{:S(2)}) collective-permute-start(bf16[128,128]{1,0:T(8,128)(2,1)} %param.72), channel_id=1, source_target_pairs={{40,0},{48,8},{56,16},{64,24},{72,32},{80,40},{88,48},{96,56},{104... | collective-permute-start | bytes 98312 | tf_op jit(solution)/shard_map/ppermute | solution.py:21
  119.7 50.4 %collective-permute-start.29 = (bf16[128,128]{1,0:T(8,128)(2,1)}, bf16[128,128]{1,0:T(8,128)(2,1)}, u32[]{:S(2)}, u32[]{:S(2)}) collective-permute-start(bf16[128,128]{1,0:T(8,128)(2,1)} %param.72), channel_id=1, source_target_pairs={{56,0},{64,8},{72,16},{80,24},{88,32},{96,40},{104,48},{112,56},{1... | collective-permute-start | bytes 98312 | tf_op jit(solution)/shard_map/ppermute | solution.py:21
  199.7 34.3 %collective-permute-start.30 = (bf16[128,128]{1,0:T(8,128)(2,1)S(1)}, bf16[128,128]{1,0:T(8,128)(2,1)S(1)}, u32[]{:S(2)}, u32[]{:S(2)}) collective-permute-start(bf16[128,128]{1,0:T(8,128)(2,1)S(1)} %get-tuple-element.950), channel_id=1, source_target_pairs={{64,0},{72,8},{80,16},{88,24},{96,32},{104,40},{112,48},{120,56},{... | collective-permute-start | bytes 98312 | tf_op jit(solution)/shard_map/ppermute | solution.py:21
  270.2 29.2 %collective-permute-start.52 = (bf16[128,128]{1,0:T(8,128)(2,1)}, bf16[128,128]{1,0:T(8,128)(2,1)}, u32[]{:S(2)}, u32[]{:S(2)}) collective-permute-start(bf16[128,128]{1,0:T(8,128)(2,1)} %get-tuple-element.973), channel_id=1, source_target_pairs={{8,0},{16,8},{24,16},{32,24},{40,32},{48,40},{56,48},{64,56},{72,6... | collective-permute-start | bytes 98312 | tf_op jit(solution)/shard_map/ppermute | solution.py:21
  272.1 31.1 %collective-permute-start.38 = (bf16[128,128]{1,0:T(8,128)(2,1)}, bf16[128,128]{1,0:T(8,128)(2,1)}, u32[]{:S(2)}, u32[]{:S(2)}) collective-permute-start(bf16[128,128]{1,0:T(8,128)(2,1)} %copy-done.44), channel_id=1, source_target_pairs={{0,8},{8,16},{16,24},{24,32},{32,40},{40,48},{48,56},{56,64},{64,7... | collective-permute-start | bytes 98312 | tf_op jit(solution)/shard_map/ppermute | solution.py:21
  276.1 30.8 %collective-permute-start.53 = (bf16[128,128]{1,0:T(8,128)(2,1)}, bf16[128,128]{1,0:T(8,128)(2,1)}, u32[]{:S(2)}, u32[]{:S(2)}) collective-permute-start(bf16[128,128]{1,0:T(8,128)(2,1)} %copy-done.43), channel_id=1, source_target_pairs={{0,8},{8,16},{16,24},{24,32},{32,40},{40,48},{48,56},{56,64},{64,7... | collective-permute-start | bytes 98312 | tf_op jit(solution)/shard_map/ppermute | solution.py:21
  278.0 40.1 %collective-permute-start.39 = (bf16[128,128]{1,0:T(8,128)(2,1)}, bf16[128,128]{1,0:T(8,128)(2,1)}, u32[]{:S(2)}, u32[]{:S(2)}) collective-permute-start(bf16[128,128]{1,0:T(8,128)(2,1)} %get-tuple-element.959), channel_id=1, source_target_pairs={{0,16},{8,24},{16,32},{24,40},{32,48},{40,56},{48,64},{56,72},{64,... | collective-permute-start | bytes 98312 | tf_op jit(solution)/shard_map/ppermute | solution.py:21
  283.9 43.3 %collective-permute-start.54 = (bf16[128,128]{1,0:T(8,128)(2,1)}, bf16[128,128]{1,0:T(8,128)(2,1)}, u32[]{:S(2)}, u32[]{:S(2)}) collective-permute-start(bf16[128,128]{1,0:T(8,128)(2,1)} %get-tuple-element.975), channel_id=1, source_target_pairs={{0,16},{8,24},{16,32},{24,40},{32,48},{40,56},{48,64},{56,72},{64,... | collective-permute-start | bytes 98312 | tf_op jit(solution)/shard_map/ppermute | solution.py:21
  299.4 35.5 %collective-permute-start.55 = (bf16[128,128]{1,0:T(8,128)(2,1)}, bf16[128,128]{1,0:T(8,128)(2,1)S(1)}, u32[]{:S(2)}, u32[]{:S(2)}) collective-permute-start(bf16[128,128]{1,0:T(8,128)(2,1)} %copy-done.45), channel_id=1, source_target_pairs={{0,24},{8,32},{16,40},{24,48},{32,56},{40,64},{48,72},{56,80},{64,... | collective-permute-start | bytes 98312 | tf_op jit(solution)/shard_map/ppermute | solution.py:21
  303.3 33.6 %collective-permute-start.56 = (bf16[128,128]{1,0:T(8,128)(2,1)}, bf16[128,128]{1,0:T(8,128)(2,1)S(1)}, u32[]{:S(2)}, u32[]{:S(2)}) collective-permute-start(bf16[128,128]{1,0:T(8,128)(2,1)} %copy-done.48), channel_id=1, source_target_pairs={{0,32},{8,40},{16,48},{24,56},{32,64},{40,72},{48,80},{56,88},{64,... | collective-permute-start | bytes 98312 | tf_op jit(solution)/shard_map/ppermute | solution.py:21
  306.9 35.0 %collective-permute-start.57 = (bf16[128,128]{1,0:T(8,128)(2,1)}, bf16[128,128]{1,0:T(8,128)(2,1)S(1)}, u32[]{:S(2)}, u32[]{:S(2)}) collective-permute-start(bf16[128,128]{1,0:T(8,128)(2,1)} %copy-done.51), channel_id=1, source_target_pairs={{0,40},{8,48},{16,56},{24,64},{32,72},{40,80},{48,88},{56,96},{64,... | collective-permute-start | bytes 98312 | tf_op jit(solution)/shard_map/ppermute | solution.py:21
  318.1 30.2 %collective-permute-start.58 = (bf16[128,128]{1,0:T(8,128)(2,1)}, bf16[128,128]{1,0:T(8,128)(2,1)S(1)}, u32[]{:S(2)}, u32[]{:S(2)}) collective-permute-start(bf16[128,128]{1,0:T(8,128)(2,1)} %copy-done.54), channel_id=1, source_target_pairs={{0,48},{8,56},{16,64},{24,72},{32,80},{40,88},{48,96},{56,104},{64... | collective-permute-start | bytes 98312 | tf_op jit(solution)/shard_map/ppermute | solution.py:21
  327.2 31.8 %collective-permute-start.59 = (bf16[128,128]{1,0:T(8,128)(2,1)}, bf16[128,128]{1,0:T(8,128)(2,1)S(1)}, u32[]{:S(2)}, u32[]{:S(2)}) collective-permute-start(bf16[128,128]{1,0:T(8,128)(2,1)} %copy-done.57), channel_id=1, source_target_pairs={{0,56},{8,64},{16,72},{24,80},{32,88},{40,96},{48,104},{56,112},{6... | collective-permute-start | bytes 98312 | tf_op jit(solution)/shard_map/ppermute | solution.py:21
  335.0 28.3 %collective-permute-start.40 = (bf16[128,128]{1,0:T(8,128)(2,1)S(1)}, bf16[128,128]{1,0:T(8,128)(2,1)S(1)}, u32[]{:S(2)}, u32[]{:S(2)}) collective-permute-start(bf16[128,128]{1,0:T(8,128)(2,1)S(1)} %copy-done.47), channel_id=1, source_target_pairs={{0,24},{8,32},{16,40},{24,48},{32,56},{40,64},{48,72},{56,80},{64,... | collective-permute-start | bytes 98312 | tf_op jit(solution)/shard_map/ppermute | solution.py:21
  336.9 26.4 %collective-permute-start.41 = (bf16[128,128]{1,0:T(8,128)(2,1)S(1)}, bf16[128,128]{1,0:T(8,128)(2,1)S(1)}, u32[]{:S(2)}, u32[]{:S(2)}) collective-permute-start(bf16[128,128]{1,0:T(8,128)(2,1)S(1)} %copy-done.50), channel_id=1, source_target_pairs={{0,32},{8,40},{16,48},{24,56},{32,64},{40,72},{48,80},{56,88},{64,... | collective-permute-start | bytes 98312 | tf_op jit(solution)/shard_map/ppermute | solution.py:21
  (97 other events, 1353.4 us)
where the time goes:
time: 373 us; the launch traced here: 369 us
  starting transfers between devices  253 us (68%)
  blocking collectives  24.8 us (7%)
  other arithmetic  23.6 us (6%)
  matrix products  19.6 us (5%)
  local copies, waits for them, and re-layouts  16.5 us (4%)
  loops' own time  14.8 us (4%)
  between operations  12.7 us (3%)
  waiting for transfers between devices  4.71 us (1%)
    ppermute x60, starting transfers between devices, shifted(): return lax.ppermute(array, axis, pairs)  253 us
    psum x1, blocking collectives, per_device(): inner = lax.psum(jnp.sum(upstream * normed, axis=-1), 'head')  12.4 us
    psum x1, blocking collectives, per_device(): square_sum = lax.psum(jnp.sum(flat * flat, axis=-1), 'head')  12.4 us
    add x11, other arithmetic, absorb(): return (new_top, row_total * rescale + weights.sum(axis=-1), numerator)  7.68 us
    another operation x16, loops' own time, per_device(): lax.cond(jnp.any(blocks > 0), partial(pair_terms, k_far, v_far), lambda u...  7.67 us
    mul x10, other arithmetic, absorb(): numerator * jnp.transpose(rescale, (2, 0, 1))[..., None] + part_sum  7.48 us
  transfers between devices with their start and end apart: 60, of which 1 were waited for; matrix products, arithmetic and copies ran while one was open for 13% of the time, Pallas kernels for 0%

commit v1 on v0

v1 whole, which is shorter than its diff:
```python
import math

import jax
import jax.numpy as jnp
from jax import lax
from jax.experimental import pallas as pl
from jax.experimental.pallas import tpu as pltpu
from jax.sharding import Mesh
from jax.sharding import PartitionSpec as P

HEADS = 32
KV_HEADS = 8
GROUP = HEADS // KV_HEADS
DH = 128
BLK = 128
ROWS = GROUP * BLK
SLOTS = 16
CHUNK = 256
NEGATIVE = -1e30
EPSILON = 1e-06
FEATURES = HEADS * DH
SCALING = DH ** (-0.5)
EXP2_SCALE = SCALING / math.log(2.0)
PAIR = ("zp", "y")
VMEM_LIMIT = 40 * 1024 * 1024


def window_slot(zp, y, peer, part):
    peer_zp, peer_y = peer // 4, peer % 4
    across = (zp - peer_zp) & 1
    shift = peer_y - y
    if part == 0:
        return 8 + shift + across * (4 * (1 - 2 * zp))
    same = shift & 15
    other = 8 + shift - 4 * (1 - 2 * zp)
    return jnp.where(across == 1, other, same)


def stacked(array):
    return jnp.concatenate([array[:, g * DH : (g + 1) * DH] for g in range(GROUP)], axis=0)


def stacked_t(array):
    return jnp.concatenate([array[:, g * DH : (g + 1) * DH].T for g in range(GROUP)], axis=1)


def unstacked_t(array):
    return jnp.concatenate([array[:, g * BLK : (g + 1) * BLK].T for g in range(GROUP)], axis=1)


def over_groups(row):
    return sum(row[:, g * BLK : (g + 1) * BLK] for g in range(GROUP))


def to_groups(row):
    return jnp.concatenate([row] * GROUP, axis=1)


def forward_kernel(place, mask, q_ref, kv_ref, up_ref, gain_ref, w_ref, att_ref, up_out, inv_ref, part_ref, s_ref):
    zp, y = place[0], place[1]
    q_t = stacked_t(q_ref[...])
    top = jnp.full((8, ROWS), NEGATIVE, jnp.float32)
    for slot in range(SLOTS):
        rows = pl.ds(slot * BLK, BLK)
        column = window_slot(zp, y, slot // 2, slot % 2)
        bias = jnp.where(mask[0, column] > 0, 0.0, NEGATIVE)
        raw = jnp.dot(kv_ref[rows, :DH], q_t, preferred_element_type=jnp.float32) + bias
        s_ref[rows, :] = raw
        top = jnp.maximum(top, raw.reshape(BLK // 8, 8, ROWS).max(axis=0))
    top = top.max(axis=0, keepdims=True)
    total = jnp.zeros((8, ROWS), jnp.float32)
    numer = jnp.zeros((DH, ROWS), jnp.float32)
    for chunk in range(SLOTS * BLK // CHUNK):
        rows = pl.ds(chunk * CHUNK, CHUNK)
        weights = jnp.exp2((s_ref[rows, :] - top) * EXP2_SCALE)
        total = total + weights.reshape(CHUNK // 8, 8, ROWS).sum(axis=0)
        rounded = weights.astype(jnp.bfloat16)
        w_ref[rows, :] = rounded
        numer = numer + jnp.dot(kv_ref[rows, DH:].T, rounded, preferred_element_type=jnp.float32)
    inverse = 1.0 / total.sum(axis=0, keepdims=True)
    attended = numer * inverse
    att_ref[...] = attended
    inv_ref[...] = jnp.broadcast_to(inverse, (8, ROWS))
    upstream = stacked_t(up_ref[...].astype(jnp.float32) * gain_ref[...])
    up_out[...] = upstream
    squares = over_groups(jnp.sum(attended * attended, axis=0, keepdims=True))
    products = over_groups(jnp.sum(upstream * attended, axis=0, keepdims=True))
    part_ref[...] = jnp.concatenate([squares, products], axis=0)


def backward_kernel(q_ref, kv_ref, w_ref, att_ref, up_ref, inv_ref, sums_ref, gain_ref, terms_ref, ds_ref, out_ref):
    sums = sums_ref[0]
    for peer in range(1, KV_HEADS):
        sums = sums + sums_ref[peer]
    root = jnp.sqrt(sums[0:1] / FEATURES + EPSILON)
    inv_root = 1.0 / root
    inner = sums[1:2] * inv_root
    attended = att_ref[...]
    normed = attended * to_groups(inv_root)
    out_ref[...] = (unstacked_t(normed) * gain_ref[...]).astype(jnp.bfloat16)
    d_att = (up_ref[...] - normed * to_groups(inner / FEATURES)) * to_groups(inv_root)
    d_att = d_att.astype(jnp.bfloat16).astype(jnp.float32)
    inverse = inv_ref[0:1]
    delta = jnp.sum(d_att * attended, axis=0, keepdims=True) * inverse
    do_t = (d_att * inverse).astype(jnp.bfloat16)
    do_rows = jnp.concatenate([do_t[:, g * BLK : (g + 1) * BLK].T for g in range(GROUP)], axis=0)
    q_rows = stacked(q_ref[...])
    for chunk in range(SLOTS * BLK // CHUNK):
        rows = pl.ds(chunk * CHUNK, CHUNK)
        weights = w_ref[rows, :]
        d_prob = jnp.dot(kv_ref[rows, DH:], do_t, preferred_element_type=jnp.float32)
        d_score = (weights.astype(jnp.float32) * (d_prob - delta)).astype(jnp.bfloat16)
        ds_ref[rows, :] = d_score
        term_k = jnp.dot(d_score, q_rows, preferred_element_type=jnp.float32) * SCALING
        term_v = jnp.dot(weights, do_rows, preferred_element_type=jnp.float32)
        terms_ref[rows, :DH] = term_k.astype(jnp.bfloat16)
        terms_ref[rows, DH:] = term_v.astype(jnp.bfloat16)


def query_kernel(kv_ref, ds_ref, grad_ref):
    grad = jnp.zeros((DH, ROWS), jnp.float32)
    for chunk in range(SLOTS * BLK // CHUNK):
        rows = pl.ds(chunk * CHUNK, CHUNK)
        grad = grad + jnp.dot(kv_ref[rows, :DH].T, ds_ref[rows, :], preferred_element_type=jnp.float32)
    grad_ref[...] = (unstacked_t(grad) * SCALING).astype(jnp.bfloat16)


def shape(dims, dtype):
    return jax.ShapeDtypeStruct(dims, dtype)


def in_vmem(count):
    return [pl.BlockSpec(memory_space=pltpu.VMEM)] * count


def in_smem(count):
    return [pl.BlockSpec(memory_space=pltpu.SMEM)] * count


def two_planes(array, by):
    length = lax.axis_size("zq")
    return lax.ppermute(array, "zq", [(i, (i + by) % length) for i in range(length)])


def per_device(queries, keys_in, values_in, norm_gain, grad_out, nearby_block_mask):
    zp, y = lax.axis_index("zp"), lax.axis_index("y")
    place = jnp.stack([zp, y]).astype(jnp.int32)
    gain = norm_gain.reshape(1, -1)
    own = jnp.concatenate([keys_in, values_in], axis=1)
    above = two_planes(own, -1)
    below = two_planes(own, 1)
    to_zp = jnp.arange(8, dtype=jnp.int32)[:, None, None] // 4
    to_y = jnp.arange(8, dtype=jnp.int32)[:, None, None] % 4
    take_below = jnp.where(to_zp == zp, y >= to_y, zp == 1)
    second = jnp.where(take_below, below[None], above[None])
    sent = jnp.stack([jnp.broadcast_to(own[None], second.shape), second], axis=1)
    gathered = lax.all_to_all(sent, PAIR, 0, 0).reshape(SLOTS * BLK, 2 * DH)

    weights, attended, upstream, inverse, part = pl.pallas_call(
        forward_kernel,
        out_shape=(
            shape((SLOTS * BLK, ROWS), jnp.bfloat16),
            shape((DH, ROWS), jnp.float32),
            shape((DH, ROWS), jnp.float32),
            shape((8, ROWS), jnp.float32),
            shape((2, BLK), jnp.float32),
        ),
        in_specs=in_smem(2) + in_vmem(4),
        out_specs=tuple(in_vmem(5)),
        scratch_shapes=[pltpu.VMEM((SLOTS * BLK, ROWS), jnp.float32)],
        compiler_params=pltpu.CompilerParams(vmem_limit_bytes=VMEM_LIMIT),
        cost_estimate=pl.CostEstimate(flops=540_000_000, bytes_accessed=4_000_000, transcendentals=1_050_000),
        name="forward",
    )(place, nearby_block_mask, queries, gathered, grad_out, gain)
    sums = lax.all_to_all(jnp.broadcast_to(part[None], (KV_HEADS, 2, BLK)), "head", 0, 0)
    terms, d_score, normed_out = pl.pallas_call(
        backward_kernel,
        out_shape=(
            shape((SLOTS * BLK, 2 * DH), jnp.bfloat16),
            shape((SLOTS * BLK, ROWS), jnp.bfloat16),
            shape((BLK, GROUP * DH), jnp.bfloat16),
        ),
        in_specs=in_vmem(8),
        out_specs=tuple(in_vmem(3)),
        compiler_params=pltpu.CompilerParams(vmem_limit_bytes=VMEM_LIMIT),
        cost_estimate=pl.CostEstimate(flops=810_000_000, bytes_accessed=6_000_000, transcendentals=0),
        name="backward",
    )(queries, gathered, weights, attended, upstream, inverse, sums, gain)
    returned = lax.all_to_all(terms.reshape(8, 2, BLK, 2 * DH), PAIR, 0, 0)
    grad_queries = pl.pallas_call(
        query_kernel,
        out_shape=shape((BLK, GROUP * DH), jnp.bfloat16),
        in_specs=in_vmem(2),
        out_specs=in_vmem(1)[0],
        compiler_params=pltpu.CompilerParams(vmem_limit_bytes=VMEM_LIMIT),
        cost_estimate=pl.CostEstimate(flops=270_000_000, bytes_accessed=3_200_000, transcendentals=0),
        name="query_grad",
    )(gathered, d_score)
    wide = returned.astype(jnp.float32)
    own_sum = wide[:, 0].sum(axis=0)
    is_below = take_below
    to_below = jnp.where(is_below, wide[:, 1], 0.0).sum(axis=0).astype(jnp.bfloat16)
    to_above = jnp.where(is_below, 0.0, wide[:, 1]).sum(axis=0).astype(jnp.bfloat16)
    from_above = two_planes(to_below, -1)
    from_below = two_planes(to_above, 1)
    total = own_sum + from_above.astype(jnp.float32) + from_below.astype(jnp.float32)
    total = total.astype(jnp.bfloat16)
    return normed_out, grad_queries, total[:, :DH], total[:, DH:]


def solution(mesh):
    spans, heads = mesh.devices.shape
    fine = Mesh(mesh.devices.reshape(spans // 8, 2, 4, heads), ("zq", "zp", "y", "head"))
    seq = ("zq", "zp", "y")
    both = P(seq, "head")
    return jax.shard_map(
        per_device,
        mesh=fine,
        in_specs=(both, both, both, P("head"), both, P(seq, None)),
        out_specs=(both, both, both, both),
        check_vma=False,
    )
```

time: 373 us -> 99 us (0.27)
  the two profiles are of different devices: /device:TPU:256 before, /device:TPU:32 now
where the time goes in v1:
time: 99 us; the launch traced here: 98.5 us
  starting transfers between devices  37.5 us (38%)
  waiting for transfers between devices  37.5 us (38%)
  blocking collectives  9.4 us (9%)
  Pallas kernels  6.98 us (7%)
  local copies, waits for them, and re-layouts  3.26 us (3%)
  other arithmetic  2.98 us (3%)
    ppermute x4, starting transfers between devices, two_planes(): lax.ppermute(array, 'zq', [(i, (i + by) % length) for i in range(length)])  26.9 us
    all_to_all x1, waiting for transfers between devices, per_device(): returned = lax.all_to_all(terms.reshape(8, 2, BLK, 2 * DH), PAIR, 0, 0)  13.4 us
    all_to_all x1, waiting for transfers between devices, per_device(): gathered = lax.all_to_all(sent, PAIR, 0, 0).reshape(SLOTS * BLK, 2 * DH)  12.6 us
    ppermute x4, waiting for transfers between devices, two_planes(): lax.ppermute(array, 'zq', [(i, (i + by) % length) for i in range(length)])  11.6 us
    all_to_all x1, blocking collectives, per_device(): lax.all_to_all(jnp.broadcast_to(part[None], (KV_HEADS, 2, BLK)), 'head',...  9.4 us
    all_to_all x1, starting transfers between devices, per_device(): gathered = lax.all_to_all(sent, PAIR, 0, 0).reshape(SLOTS * BLK, 2 * DH)  5.93 us
    all_to_all x1, starting transfers between devices, per_device(): returned = lax.all_to_all(terms.reshape(8, 2, BLK, 2 * DH), PAIR, 0, 0)  4.74 us
    pallas_call x1, Pallas kernels, per_device(): pl.pallas_call(backward_kernel, out_shape=(shape((SLOTS * BLK, 2 * DH), j...  3.07 us
  transfers between devices with their start and end apart: 6, of which 5 were waited for; matrix products, arithmetic and copies ran while one was open for 0% of the time, Pallas kernels for 1%

profile of v1, /device:TPU:32, one launch (start us, length us, event | category | flops | bytes accessed | tf_op | source)
XLA Modules:
  0.0 98.5 jit_solution(6169817731431705027)
XLA Ops:
  0.6 0.8 constant_dynamic-update-slice_fusion.1
  1.4 0.8 constant_dynamic-update-slice_fusion
  2.2 18.2 %collective-permute-start.1 = (bf16[128,256]{1,0:T(8,128)(2,1)S(1)}, bf16[128,256]{1,0:T(8,128)(2,1)S(1)}, u32[]{:S(2)}, u32[]{:S(2)}) collective-permute-start(bf16[128,256]{1,0:T(8,128)(2,1)S(1)} %constant_dynamic-update-slice_fusion), channel_id=1, source_target_pairs={{0,960},{64,0},{128,64},{192,128},{256,192},{320,256},{384,320},{4... | collective-permute-start | bytes 196616 | tf_op jit(solution)/shard_map/ppermute | solution.py:142
  20.4 1.9 %collective-permute-start = (bf16[128,256]{1,0:T(8,128)(2,1)S(1)}, bf16[128,256]{1,0:T(8,128)(2,1)S(1)}, u32[]{:S(2)}, u32[]{:S(2)}) collective-permute-start(bf16[128,256]{1,0:T(8,128)(2,1)S(1)} %constant_dynamic-update-slice_fusion), channel_id=1, source_target_pairs={{0,64},{64,128},{128,192},{192,256},{256,320},{320,384},{384,448},... | collective-permute-start | bytes 196616 | tf_op jit(solution)/shard_map/ppermute | solution.py:142
  22.3 7.1 %collective-permute-done = bf16[128,256]{1,0:T(8,128)(2,1)S(1)} collective-permute-done((bf16[128,256]{1,0:T(8,128)(2,1)S(1)}, bf16[128,256]{1,0:T(8,128)(2,1)S(1)}, u32[]{:S(2)}, u32[]{:S(2)}) %collective-permute-start) | collective-permute-done | bytes 65568 | tf_op jit(solution)/shard_map/ppermute | solution.py:142
  29.5 0.1 broadcast_select_fusion
  29.7 1.1 %pad_maximum_fusion = bf16[8,2,128,256]{3,2,1,0:T(8,128)(2,1)} fusion(bf16[8,1,128,256]{3,2,1,0:T(8,128)(2,1)S(1)} %broadcast_select_fusion, bf16[8,1,128,256]{3,2,1,0:T(8,128)(2,1)S(1)} %stack_broadcast_in_dim.2), kind=kLoop, calls=%fused_computation.2 | loop fusion | flops 524288 | bytes 2097152 | tf_op jit(solution)/shard_map/stack | solution.py:156
  30.7 5.9 %all-to-all-start = ((bf16[8,2,128,256]{3,2,1,0:T(8,128)(2,1)}), bf16[8,2,128,256]{3,2,1,0:T(8,128)(2,1)S(1)}, u32[]{:S(2)}, u32[]{:S(2)}) async-start(bf16[8,2,128,256]{3,2,1,0:T(8,128)(2,1)} %pad_maximum_fusion), calls=%async_computation | async-start | bytes 2097152 | tf_op jit(solution)/shard_map/all_to_all | solution.py:157
  36.6 0.1 pad_add_fusion.place
  36.7 12.6 %all-to-all-done = bf16[8,2,128,256]{3,2,1,0:T(8,128)(2,1)S(1)} async-done(((bf16[8,2,128,256]{3,2,1,0:T(8,128)(2,1)}), bf16[8,2,128,256]{3,2,1,0:T(8,128)(2,1)S(1)}, u32[]{:S(2)}, u32[]{:S(2)}) %all-to-all-start) | async-done | bytes 1048608 | tf_op jit(solution)/shard_map/all_to_all | solution.py:157
  49.3 2.7 %forward.1 = (bf16[2048,512]{1,0:T(8,128)(2,1)S(1)}, f32[128,512]{1,0:T(8,128)S(1)}, f32[128,512]{1,0:T(8,128)S(1)}, f32[8,512]{1,0:T(8,128)S(1)}, f32[2,128]{1,0:T(2,128)S(1)}) custom-call(s32[2]{0:T(128)S(1)} %pad_add_fusion.place, s32[1,16]{1,0:T(1,128)S(1)} %copy-done.4, bf16[128,512]{1,0:T(8,128)(2,1)S(1)} %copy-done.1, bf16[2048,256]{1,0:T(8,128)(2,1)S(1)} %bitcast.11, ...), custom_call_target="tpu_custom_call" | custom-call | flops 540000000 | bytes 4000000 | tf_op jit(solution)/shard_map/forward/pallas_call | solution.py:159
  52.0 9.4 %all_to_all.15.sums_ref = f32[8,2,128]{2,1,0:T(2,128)S(1)} all-to-all(f32[8,2,128]{2,1,0:T(2,128)S(1)} %broadcast_in_dim.63), channel_id=1, replica_groups=mesh['zq'=16,'zp'=2,'y'=4,'head'=8] {'head'}, dimensions={0} | all-to-all | bytes 16384 | tf_op jit(solution)/shard_map/all_to_all | solution.py:175
  61.4 3.1 %backward.1 = (bf16[2048,256]{1,0:T(8,128)(2,1)S(1)}, bf16[2048,512]{1,0:T(8,128)(2,1)S(1)}, bf16[128,512]{1,0:T(8,128)(2,1)}) custom-call(bf16[128,512]{1,0:T(8,128)(2,1)S(1)} %copy-done.1, bf16[2048,256]{1,0:T(8,128)(2,1)S(1)} %bitcast.12, bf16[2048,512]{1,0:T(8,128)(2,1)S(1)} %get-tuple-element.12.w_ref, f32[128,512]{1,0:T(8,128)S(1)} %get-tuple-element.13.att_ref, ...), custom_call_target="tpu_custom_call" | custom-call | flops 810000000 | bytes 6000000 | tf_op jit(solution)/shard_map/backward/pallas_call | solution.py:176
  64.5 1.0 %copy-done = bf16[2048,256]{1,0:T(8,128)(2,1)} copy-done((bf16[2048,256]{1,0:T(8,128)(2,1)}, bf16[2048,256]{1,0:T(8,128)(2,1)S(1)}, u32[]{:S(2)}) %copy-start) | copy-done | bytes 1048600
  65.5 4.7 %all-to-all-start.2 = ((bf16[8,2,128,256]{3,2,1,0:T(8,128)(2,1)}), bf16[8,2,128,256]{3,2,1,0:T(8,128)(2,1)}, u32[]{:S(2)}, u32[]{:S(2)}) async-start(bf16[8,2,128,256]{3,2,1,0:T(8,128)(2,1)} %bitcast.14), calls=%async_computation.2 | async-start | bytes 2097152 | tf_op jit(solution)/shard_map/all_to_all | solution.py:189
  70.2 1.2 %query_grad.1 = bf16[128,512]{1,0:T(8,128)(2,1)} custom-call(bf16[2048,256]{1,0:T(8,128)(2,1)S(1)} %bitcast.13, bf16[2048,512]{1,0:T(8,128)(2,1)S(1)} %get-tuple-element.18.ds_ref), custom_call_target="tpu_custom_call" | custom-call | flops 270000000 | bytes 3200000 | tf_op jit(solution)/shard_map/query_grad/pallas_call | solution.py:190
  71.5 13.4 %all-to-all-done.2 = bf16[8,2,128,256]{3,2,1,0:T(8,128)(2,1)} async-done(((bf16[8,2,128,256]{3,2,1,0:T(8,128)(2,1)}), bf16[8,2,128,256]{3,2,1,0:T(8,128)(2,1)}, u32[]{:S(2)}, u32[]{:S(2)}) %all-to-all-start.2) | async-done | bytes 1048608 | tf_op jit(solution)/shard_map/all_to_all | solution.py:189
  84.8 1.4 %convert_element_type.18 = f32[8,2,128,256]{3,2,1,0:T(8,128)S(1)} convert(bf16[8,2,128,256]{3,2,1,0:T(8,128)(2,1)} %all-to-all-done.2) | non-fusion elementwise | flops 524288 | bytes 3145728 | tf_op jit(solution)/shard_map/convert_element_type | solution.py:199
  86.3 0.2 select_reduce_fusion.1
  86.5 2.4 %collective-permute-start.2 = (bf16[128,256]{1,0:T(8,128)(2,1)S(1)}, bf16[128,256]{1,0:T(8,128)(2,1)S(1)}, u32[]{:S(2)}, u32[]{:S(2)}) collective-permute-start(bf16[128,256]{1,0:T(8,128)(2,1)S(1)} %get-tuple-element.20), channel_id=1, source_target_pairs={{0,960},{64,0},{128,64},{192,128},{256,192},{320,256},{384,320},{4... | collective-permute-start | bytes 196616 | tf_op jit(solution)/shard_map/ppermute | solution.py:142
  88.9 4.3 %collective-permute-start.3 = (bf16[128,256]{1,0:T(8,128)(2,1)S(1)}, bf16[128,256]{1,0:T(8,128)(2,1)S(1)}, u32[]{:S(2)}, u32[]{:S(2)}) collective-permute-start(bf16[128,256]{1,0:T(8,128)(2,1)S(1)} %get-tuple-element.21), channel_id=1, source_target_pairs={{0,64},{64,128},{128,192},{192,256},{256,320},{320,384},{384,448},... | collective-permute-start | bytes 196616 | tf_op jit(solution)/shard_map/ppermute | solution.py:142
  93.3 0.5 collective-permute-done.2
  93.8 4.1 %collective-permute-done.3 = bf16[128,256]{1,0:T(8,128)(2,1)S(1)} collective-permute-done((bf16[128,256]{1,0:T(8,128)(2,1)S(1)}, bf16[128,256]{1,0:T(8,128)(2,1)S(1)}, u32[]{:S(2)}, u32[]{:S(2)}) %collective-permute-start.3) | collective-permute-done | bytes 65568 | tf_op jit(solution)/shard_map/ppermute | solution.py:142
  97.9 0.6 fusion
  (15 shorter events, 0.2 us)
Async XLA Ops:
  2.2 20.2 %collective-permute-start.1 = (bf16[128,256]{1,0:T(8,128)(2,1)S(1)}, bf16[128,256]{1,0:T(8,128)(2,1)S(1)}, u32[]{:S(2)}, u32[]{:S(2)}) collective-permute-start(bf16[128,256]{1,0:T(8,128)(2,1)S(1)} %constant_dynamic-update-slice_fusion), channel_id=1, source_target_pairs={{0,960},{64,0},{128,64},{192,128},{256,192},{320,256},{384,320},{4... | collective-permute-start | bytes 196616 | tf_op jit(solution)/shard_map/ppermute | solution.py:142
  20.4 9.1 %collective-permute-start = (bf16[128,256]{1,0:T(8,128)(2,1)S(1)}, bf16[128,256]{1,0:T(8,128)(2,1)S(1)}, u32[]{:S(2)}, u32[]{:S(2)}) collective-permute-start(bf16[128,256]{1,0:T(8,128)(2,1)S(1)} %constant_dynamic-update-slice_fusion), channel_id=1, source_target_pairs={{0,64},{64,128},{128,192},{192,256},{256,320},{320,384},{384,448},... | collective-permute-start | bytes 196616 | tf_op jit(solution)/shard_map/ppermute | solution.py:142
  29.6 19.7 %copy-start.1 = (bf16[128,512]{1,0:T(8,128)(2,1)S(1)}, bf16[128,512]{1,0:T(8,128)(2,1)}, u32[]{:S(2)}) copy-start(bf16[128,512]{1,0:T(8,128)(2,1)} %q_ref.3) | copy-start | bytes 393220
  29.6 19.7 %copy-start.2 = (f32[512]{0:T(512)S(1)}, f32[512]{0:T(512)}, u32[]{:S(2)}) copy-start(f32[512]{0:T(512)} %param.9) | copy-start | bytes 6148
  29.6 19.6 %copy-start.3 = (bf16[128,512]{1,0:T(8,128)(2,1)S(1)}, bf16[128,512]{1,0:T(8,128)(2,1)}, u32[]{:S(2)}) copy-start(bf16[128,512]{1,0:T(8,128)(2,1)} %up_ref.1) | copy-start | bytes 393220
  29.6 19.6 %copy-start.4 = (s32[1,16]{1,0:T(1,128)S(1)}, s32[1,16]{1,0:T(1,128)}, u32[]{:S(2)}) copy-start(s32[1,16]{1,0:T(1,128)} %mask.1) | copy-start | bytes 196
  30.7 18.6 %all-to-all-start = ((bf16[8,2,128,256]{3,2,1,0:T(8,128)(2,1)}), bf16[8,2,128,256]{3,2,1,0:T(8,128)(2,1)S(1)}, u32[]{:S(2)}, u32[]{:S(2)}) async-start(bf16[8,2,128,256]{3,2,1,0:T(8,128)(2,1)} %pad_maximum_fusion), calls=%async_computation | async-start | bytes 2097152 | tf_op jit(solution)/shard_map/all_to_all | solution.py:157
  64.5 1.0 %copy-start = (bf16[2048,256]{1,0:T(8,128)(2,1)}, bf16[2048,256]{1,0:T(8,128)(2,1)S(1)}, u32[]{:S(2)}) copy-start(bf16[2048,256]{1,0:T(8,128)(2,1)S(1)} %get-tuple-element.19) | copy-start | bytes 3145732
  65.5 19.3 %all-to-all-start.2 = ((bf16[8,2,128,256]{3,2,1,0:T(8,128)(2,1)}), bf16[8,2,128,256]{3,2,1,0:T(8,128)(2,1)}, u32[]{:S(2)}, u32[]{:S(2)}) async-start(bf16[8,2,128,256]{3,2,1,0:T(8,128)(2,1)} %bitcast.14), calls=%async_computation.2 | async-start | bytes 2097152 | tf_op jit(solution)/shard_map/all_to_all | solution.py:189
  86.5 7.3 %collective-permute-start.2 = (bf16[128,256]{1,0:T(8,128)(2,1)S(1)}, bf16[128,256]{1,0:T(8,128)(2,1)S(1)}, u32[]{:S(2)}, u32[]{:S(2)}) collective-permute-start(bf16[128,256]{1,0:T(8,128)(2,1)S(1)} %get-tuple-element.20), channel_id=1, source_target_pairs={{0,960},{64,0},{128,64},{192,128},{256,192},{320,256},{384,320},{4... | collective-permute-start | bytes 196616 | tf_op jit(solution)/shard_map/ppermute | solution.py:142
  88.9 8.9 %collective-permute-start.3 = (bf16[128,256]{1,0:T(8,128)(2,1)S(1)}, bf16[128,256]{1,0:T(8,128)(2,1)S(1)}, u32[]{:S(2)}, u32[]{:S(2)}) collective-permute-start(bf16[128,256]{1,0:T(8,128)(2,1)S(1)} %get-tuple-element.21), channel_id=1, source_target_pairs={{0,64},{64,128},{128,192},{192,256},{256,320},{320,384},{384,448},... | collective-permute-start | bytes 196616 | tf_op jit(solution)/shard_map/ppermute | solution.py:142

commit v2 on v1

v2 whole, which is shorter than its diff:
```python
import math

import jax
import jax.numpy as jnp
from jax import lax
from jax.experimental import pallas as pl
from jax.experimental.pallas import tpu as pltpu
from jax.sharding import Mesh
from jax.sharding import PartitionSpec as P

HEADS = 32
KV_HEADS = 8
GROUP = HEADS // KV_HEADS
DH = 128
BLK = 128
ROWS = GROUP * BLK
PEERS = 8
NEGATIVE = -1e30
EPSILON = 1e-06
FEATURES = HEADS * DH
SCALING = DH ** (-0.5)
EXP2_SCALE = SCALING / math.log(2.0)
PAIR = ("zp", "y")
VMEM_LIMIT = 12 * 1024 * 1024


def window_slot(zp, y, peer, part):
    peer_zp, peer_y = peer // 4, peer % 4
    across = (zp - peer_zp) & 1
    shift = peer_y - y
    if part == 0:
        return 8 + shift + across * (4 * (1 - 2 * zp))
    same = shift & 15
    other = 8 + shift - 4 * (1 - 2 * zp)
    return jnp.where(across == 1, other, same)


def stacked(array):
    return jnp.concatenate([array[:, g * DH : (g + 1) * DH] for g in range(GROUP)], axis=0)


def stacked_t(array):
    return jnp.concatenate([array[:, g * DH : (g + 1) * DH].T for g in range(GROUP)], axis=1)


def unstacked_t(array):
    return jnp.concatenate([array[:, g * BLK : (g + 1) * BLK].T for g in range(GROUP)], axis=1)


def over_groups(row):
    return sum(row[:, g * BLK : (g + 1) * BLK] for g in range(GROUP))


def to_groups(row):
    return jnp.concatenate([row] * GROUP, axis=1)


def forward_half(part, place, mask, q_t, kv_ref, w_ref, s_ref):
    zp, y = place[0], place[1]
    top = jnp.full((8, ROWS), NEGATIVE, jnp.float32)
    for peer in range(PEERS):
        bias = jnp.where(mask[0, window_slot(zp, y, peer, part)] > 0, 0.0, NEGATIVE)
        raw = jnp.dot(kv_ref[peer, 0], q_t, preferred_element_type=jnp.float32) + bias
        s_ref[peer] = raw
        top = jnp.maximum(top, raw.reshape(BLK // 8, 8, ROWS).max(axis=0))
    top = top.max(axis=0, keepdims=True)
    total = jnp.zeros((8, ROWS), jnp.float32)
    numer = jnp.zeros((DH, ROWS), jnp.float32)
    for peer in range(PEERS):
        weights = jnp.exp2((s_ref[peer] - top) * EXP2_SCALE)
        total = total + weights.reshape(BLK // 8, 8, ROWS).sum(axis=0)
        rounded = weights.astype(jnp.bfloat16)
        w_ref[peer] = rounded
        numer = numer + jnp.dot(kv_ref[peer, 1].T, rounded, preferred_element_type=jnp.float32)
    return top, total.sum(axis=0, keepdims=True), numer


def near_kernel(place, mask, q_ref, kv_ref, up_ref, gain_ref, w_ref, num_ref, up_out, stat_ref, s_ref):
    q_t = stacked_t(q_ref[...])
    top, total, numer = forward_half(0, place, mask, q_t, kv_ref, w_ref, s_ref)
    num_ref[...] = numer
    stat_ref[...] = jnp.concatenate([top, total] * 4, axis=0)
    up_out[...] = stacked_t(up_ref[...].astype(jnp.float32) * gain_ref[...])


def far_kernel(place, mask, q_ref, kv_ref, num_ref, up_ref, stat_ref, w_ref, att_ref, inv_ref, part_ref, s_ref):
    q_t = stacked_t(q_ref[...])
    top, total, numer = forward_half(1, place, mask, q_t, kv_ref, w_ref, s_ref)
    near_top, near_total = stat_ref[0:1], stat_ref[1:2]
    both = jnp.maximum(top, near_top)
    far_scale = jnp.exp2((top - both) * EXP2_SCALE)
    near_scale = jnp.exp2((near_top - both) * EXP2_SCALE)
    inverse = 1.0 / (total * far_scale + near_total * near_scale)
    far_scale, near_scale = far_scale * inverse, near_scale * inverse
    attended = numer * far_scale + num_ref[...] * near_scale
    att_ref[...] = attended
    inv_ref[...] = jnp.concatenate([near_scale, far_scale] * 4, axis=0)
    squares = over_groups(jnp.sum(attended * attended, axis=0, keepdims=True))
    products = over_groups(jnp.sum(up_ref[...] * attended, axis=0, keepdims=True))
    part_ref[...] = jnp.concatenate([squares, products], axis=0)


def scaled_upstream(d_att, delta, inverse):
    delta = delta * inverse
    do_t = (d_att * inverse).astype(jnp.bfloat16)
    return do_t, delta


def score_grad(values, weights, do_t, delta):
    d_prob = jnp.dot(values, do_t, preferred_element_type=jnp.float32)
    return (weights.astype(jnp.float32) * (d_prob - delta)).astype(jnp.bfloat16)


def send_terms(peer, weights, d_score, do_rows, q_rows, terms_ref, held, sent):
    term_k = jnp.dot(d_score, q_rows, preferred_element_type=jnp.float32) * SCALING
    term_v = jnp.dot(weights, do_rows, preferred_element_type=jnp.float32)
    held[peer, 0] = term_k.astype(jnp.bfloat16)
    held[peer, 1] = term_v.astype(jnp.bfloat16)
    copy = pltpu.make_async_copy(held.at[peer], terms_ref.at[peer], sent.at[peer])
    copy.start()
    return copy


def rows_of(do_t):
    return jnp.concatenate([do_t[:, g * BLK : (g + 1) * BLK].T for g in range(GROUP)], axis=0)


def far_back_kernel(q_ref, kv_ref, w_ref, att_ref, up_ref, inv_ref, sums_ref, terms_ref, do_ref, delta_ref, root_ref, held, sent):
    sums = sums_ref[0]
    for peer in range(1, KV_HEADS):
        sums = sums + sums_ref[peer]
    root = jnp.sqrt(sums[0:1] / FEATURES + EPSILON)
    inv_root = 1.0 / root
    inner = sums[1:2] * inv_root
    attended = att_ref[...]
    normed = attended * to_groups(inv_root)
    d_att = (up_ref[...] - normed * to_groups(inner / FEATURES)) * to_groups(inv_root)
    d_att = d_att.astype(jnp.bfloat16)
    do_ref[...] = d_att
    d_att = d_att.astype(jnp.float32)
    delta = jnp.sum(d_att * attended, axis=0, keepdims=True)
    delta_ref[...] = jnp.broadcast_to(delta, (8, ROWS))
    root_ref[...] = jnp.broadcast_to(inv_root, (8, BLK))
    do_t, delta = scaled_upstream(d_att, delta, inv_ref[1:2])
    do_rows = rows_of(do_t)
    q_rows = stacked(q_ref[...])
    copies = []
    for peer in range(PEERS):
        weights = w_ref[peer]
        d_score = score_grad(kv_ref[peer, 1], weights, do_t, delta)
        copies.append(send_terms(peer, weights, d_score, do_rows, q_rows, terms_ref, held, sent))
    for copy in copies:
        copy.wait()


def near_back_kernel(
    q_ref, near_ref, far_ref, w_near_ref, w_far_ref, inv_ref, do_ref, delta_ref, att_ref, root_ref, gain_ref,
    terms_ref, grad_ref, out_ref, held, sent,
):
    d_att = do_ref[...].astype(jnp.float32)
    do_t, delta = scaled_upstream(d_att, delta_ref[0:1], inv_ref[0:1])
    do_rows = rows_of(do_t)
    q_rows = stacked(q_ref[...])
    grad = jnp.zeros((DH, ROWS), jnp.float32)
    copies = []
    for peer in range(PEERS):
        weights = w_near_ref[peer]
        d_score = score_grad(near_ref[peer, 1], weights, do_t, delta)
        copies.append(send_terms(peer, weights, d_score, do_rows, q_rows, terms_ref, held, sent))
        grad = grad + jnp.dot(near_ref[peer, 0].T, d_score, preferred_element_type=jnp.float32)
    do_t, delta = scaled_upstream(d_att, delta_ref[0:1], inv_ref[1:2])
    for peer in range(PEERS):
        d_score = score_grad(far_ref[peer, 1], w_far_ref[peer], do_t, delta)
        grad = grad + jnp.dot(far_ref[peer, 0].T, d_score, preferred_element_type=jnp.float32)
    grad_ref[...] = (unstacked_t(grad) * SCALING).astype(jnp.bfloat16)
    normed = att_ref[...] * to_groups(root_ref[0:1])
    out_ref[...] = (unstacked_t(normed) * gain_ref[...]).astype(jnp.bfloat16)
    for copy in copies:
        copy.wait()


def sums_kernel(place, far_ref, below_ref, above_ref):
    zp, y = place[0], place[1]
    below = jnp.zeros((2, BLK, DH), jnp.float32)
    above = jnp.zeros((2, BLK, DH), jnp.float32)
    for peer in range(PEERS):
        take = jnp.where(zp == peer // 4, y >= peer % 4, zp == 1)
        share = jnp.where(take, 1.0, 0.0)
        term = far_ref[peer].astype(jnp.float32)
        below = below + term * share
        above = above + term * (1.0 - share)
    below_ref[...] = below.astype(jnp.bfloat16)
    above_ref[...] = above.astype(jnp.bfloat16)


def last_kernel(near_ref, below_ref, above_ref, keys_ref, values_ref):
    total = below_ref[...].astype(jnp.float32) + above_ref[...].astype(jnp.float32)
    for peer in range(PEERS):
        total = total + near_ref[peer].astype(jnp.float32)
    keys_ref[...] = total[0].astype(jnp.bfloat16)
    values_ref[...] = total[1].astype(jnp.bfloat16)


def shape(dims, dtype):
    return jax.ShapeDtypeStruct(dims, dtype)


def in_vmem(count):
    return [pl.BlockSpec(memory_space=pltpu.VMEM)] * count


def in_smem(count):
    return [pl.BlockSpec(memory_space=pltpu.SMEM)] * count


def two_planes(array, by):
    length = lax.axis_size("zq")
    return lax.ppermute(array, "zq", [(i, (i + by) % length) for i in range(length)])


def call(kernel, name, outs, smem, vmem, scratch=(), flops=0, size=0, hbm=0):
    specs = tuple([pl.BlockSpec(memory_space=pltpu.HBM)] * hbm + in_vmem(len(outs) - hbm))
    return pl.pallas_call(
        kernel,
        out_shape=tuple(pltpu.HBM(o.shape, o.dtype) for o in outs[:hbm]) + tuple(outs[hbm:]),
        in_specs=in_smem(smem) + in_vmem(vmem),
        out_specs=specs,
        scratch_shapes=list(scratch),
        compiler_params=pltpu.CompilerParams(vmem_limit_bytes=VMEM_LIMIT),
        cost_estimate=pl.CostEstimate(flops=flops, bytes_accessed=size, transcendentals=0),
        name=name,
    )


def per_device(queries, keys_in, values_in, norm_gain, grad_out, nearby_block_mask):
    zp, y = lax.axis_index("zp"), lax.axis_index("y")
    place = jnp.stack([zp, y]).astype(jnp.int32)
    gain = norm_gain.reshape(1, -1)
    bf16, f32 = jnp.bfloat16, jnp.float32
    block = (2, BLK, DH)
    blocks = shape((PEERS, 2, BLK, DH), bf16)
    squares = shape((PEERS, BLK, ROWS), bf16)
    columns = shape((DH, ROWS), f32)
    row = shape((8, ROWS), f32)

    first = jnp.arange(2, dtype=jnp.int32)[:, None, None] == 0
    own = jnp.where(first, keys_in[None], values_in[None])
    above = two_planes(own, -1)
    below = two_planes(own, 1)
    near = lax.all_to_all(jnp.broadcast_to(own[None], (PEERS,) + block), PAIR, 0, 0)
    to_zp = jnp.arange(PEERS, dtype=jnp.int32)[:, None, None, None] // 4
    to_y = jnp.arange(PEERS, dtype=jnp.int32)[:, None, None, None] % 4
    take_below = jnp.where(to_zp == zp, y >= to_y, zp == 1)
    far = lax.all_to_all(jnp.where(take_below, below[None], above[None]), PAIR, 0, 0)

    sending = [pltpu.VMEM((PEERS,) + block, bf16), pltpu.SemaphoreType.DMA((PEERS,))]
    scores = [pltpu.VMEM((PEERS, BLK, ROWS), f32)]
    w_near, numer, upstream, stats = call(
        near_kernel, "near", (squares, columns, columns, row), 2, 4, scores, 280_000_000, 3_000_000
    )(place, nearby_block_mask, queries, near, grad_out, gain)
    w_far, attended, inverse, part = call(
        far_kernel, "far", (squares, columns, row, shape((2, BLK), f32)), 2, 5, scores, 280_000_000, 3_000_000
    )(place, nearby_block_mask, queries, far, numer, upstream, stats)
    sums = lax.all_to_all(jnp.broadcast_to(part[None], (KV_HEADS, 2, BLK)), "head", 0, 0)
    far_terms, d_att, delta, inv_root = call(
        far_back_kernel,
        "far_back",
        (blocks, shape((DH, ROWS), bf16), row, shape((8, BLK), f32)),
        0, 7, sending, 400_000_000, 4_000_000, 1,
    )(queries, far, w_far, attended, upstream, inverse, sums)
    far_back = lax.all_to_all(far_terms, PAIR, 0, 0)
    tall = shape((BLK, GROUP * DH), bf16)
    near_terms, grad_queries, normed_out = call(
        near_back_kernel, "near_back", (blocks, tall, tall), 0, 11, sending, 800_000_000, 6_000_000, 1
    )(queries, near, far, w_near, w_far, inverse, d_att, delta, attended, inv_root, gain)
    near_back = lax.all_to_all(near_terms, PAIR, 0, 0)
    half = shape(block, bf16)
    to_below, to_above = call(sums_kernel, "sums", (half, half), 1, 1, (), 1_000_000, 600_000)(place, far_back)
    from_above = two_planes(to_below, -1)
    from_below = two_planes(to_above, 1)
    piece = shape((BLK, DH), bf16)
    grad_keys, grad_values = call(last_kernel, "last", (piece, piece), 0, 3, (), 1_000_000, 700_000)(
        near_back, from_below, from_above
    )
    return normed_out, grad_queries, grad_keys, grad_values


def solution(mesh):
    spans, heads = mesh.devices.shape
    fine = Mesh(mesh.devices.reshape(spans // 8, 2, 4, heads), ("zq", "zp", "y", "head"))
    seq = ("zq", "zp", "y")
    both = P(seq, "head")
    return jax.shard_map(
        per_device,
        mesh=fine,
        in_specs=(both, both, both, P("head"), both, P(seq, None)),
        out_specs=(both, both, both, both),
        check_vma=False,
    )
```

time: 99 us -> 93.7 us (0.946)
  the two profiles are of different devices: /device:TPU:32 before, /device:TPU:8 now
where the time goes in v2:
time: 93.7 us; the launch traced here: 93 us
  starting transfers between devices  50.1 us (53%)
  waiting for transfers between devices  14.6 us (16%)
  Pallas kernels  12.5 us (13%)
  blocking collectives  9.41 us (10%)
  local copies, waits for them, and re-layouts  3.78 us (4%)
  other arithmetic  1.85 us (2%)
    ppermute x4, starting transfers between devices, two_planes(): lax.ppermute(array, 'zq', [(i, (i + by) % length) for i in range(length)])  17.9 us
    all_to_all x1, starting transfers between devices, per_device(): lax.all_to_all(jnp.broadcast_to(own[None], (PEERS,) + block), PAIR, 0, 0)  16.5 us
    all_to_all x1, blocking collectives, per_device(): lax.all_to_all(jnp.broadcast_to(part[None], (KV_HEADS, 2, BLK)), 'head',...  9.41 us
    ppermute x4, waiting for transfers between devices, two_planes(): lax.ppermute(array, 'zq', [(i, (i + by) % length) for i in range(length)])  9.15 us
    all_to_all x1, starting transfers between devices, per_device(): lax.all_to_all(jnp.where(take_below, below[None], above[None]), PAIR, 0, 0)  5.86 us
    all_to_all x1, starting transfers between devices, per_device(): far_back = lax.all_to_all(far_terms, PAIR, 0, 0)  5.07 us
    all_to_all x1, starting transfers between devices, per_device(): near_back = lax.all_to_all(near_terms, PAIR, 0, 0)  4.83 us
    pallas_call x1, Pallas kernels, per_device(): call(near_back_kernel, 'near_back', (blocks, tall, tall), 0, 11, sending,...  4.64 us
  transfers between devices with their start and end apart: 8, of which 5 were waited for; matrix products, arithmetic and copies ran while one was open for 1% of the time, Pallas kernels for 8%

profile of v2, /device:TPU:8, one launch (start us, length us, event | category | flops | bytes accessed | tf_op | source)
XLA Modules:
  0.0 93.0 jit_solution(10587045215282188900)
XLA Ops:
  0.6 0.9 broadcast_select_fusion.1
  1.5 0.9 broadcast_in_dim.74
  2.4 16.5 %all-to-all-start = ((bf16[8,2,128,128]{3,2,1,0:T(8,128)(2,1)}), bf16[8,2,128,128]{3,2,1,0:T(8,128)(2,1)S(1)}, u32[]{:S(2)}, u32[]{:S(2)}) async-start(bf16[8,2,128,128]{3,2,1,0:T(8,128)(2,1)} %broadcast_in_dim.74), calls=%async_computation | async-start | bytes 1048576 | tf_op jit(solution)/shard_map/all_to_all | solution.py:250
  18.9 8.0 %collective-permute-start.1 = (bf16[2,128,128]{2,1,0:T(8,128)(2,1)S(1)}, bf16[2,128,128]{2,1,0:T(8,128)(2,1)S(1)}, u32[]{:S(2)}, u32[]{:S(2)}) collective-permute-start(bf16[2,128,128]{2,1,0:T(8,128)(2,1)S(1)} %broadcast_select_fusion.1), channel_id=1, source_target_pairs={{0,960},{64,0},{128,64},{192,128},{256,192},{320,256},{384,320},{4... | collective-permute-start | bytes 196616 | tf_op jit(solution)/shard_map/ppermute | solution.py:218
  26.9 1.9 %collective-permute-start = (bf16[2,128,128]{2,1,0:T(8,128)(2,1)S(1)}, bf16[2,128,128]{2,1,0:T(8,128)(2,1)S(1)}, u32[]{:S(2)}, u32[]{:S(2)}) collective-permute-start(bf16[2,128,128]{2,1,0:T(8,128)(2,1)S(1)} %broadcast_select_fusion.1), channel_id=1, source_target_pairs={{0,64},{64,128},{128,192},{192,256},{256,320},{320,384},{384,448},... | collective-permute-start | bytes 196616 | tf_op jit(solution)/shard_map/ppermute | solution.py:218
  28.8 7.0 %collective-permute-done = bf16[2,128,128]{2,1,0:T(8,128)(2,1)S(1)} collective-permute-done((bf16[2,128,128]{2,1,0:T(8,128)(2,1)S(1)}, bf16[2,128,128]{2,1,0:T(8,128)(2,1)S(1)}, u32[]{:S(2)}, u32[]{:S(2)}) %collective-permute-start) | collective-permute-done | bytes 65568 | tf_op jit(solution)/shard_map/ppermute | solution.py:218
  35.8 0.9 broadcast_select_fusion
  36.7 5.9 %all-to-all-start.1 = ((bf16[8,2,128,128]{3,2,1,0:T(8,128)(2,1)}), bf16[8,2,128,128]{3,2,1,0:T(8,128)(2,1)S(1)}, u32[]{:S(2)}, u32[]{:S(2)}) async-start(bf16[8,2,128,128]{3,2,1,0:T(8,128)(2,1)} %broadcast_select_fusion), calls=%async_computation.1 | async-start | bytes 1048576 | tf_op jit(solution)/shard_map/all_to_all | solution.py:254
  43.3 1.9 %near.1 = (bf16[8,128,512]{2,1,0:T(8,128)(2,1)S(1)}, f32[128,512]{1,0:T(8,128)S(1)}, f32[128,512]{1,0:T(8,128)S(1)}, f32[8,512]{1,0:T(8,128)S(1)}) custom-call(s32[2]{0:T(128)S(1)} %pad_add_fusion.place, s32[1,16]{1,0:T(1,128)S(1)} %copy-done.4, bf16[128,512]{1,0:T(8,128)(2,1)S(1)} %copy-done, bf16[8,2,128,128]{3,2,1,0:T(8,128)(2,1)S(1)} %all-to-all-done.kv_ref.near_ref, ...), custom_call_target="tpu_custom_call" | custom-call | flops 280000000 | bytes 3000000 | tf_op jit(solution)/shard_map/near/pallas_call | solution.py:258
  45.2 1.0 %copy-done.1 = bf16[8,128,512]{2,1,0:T(8,128)(2,1)} copy-done((bf16[8,128,512]{2,1,0:T(8,128)(2,1)}, bf16[8,128,512]{2,1,0:T(8,128)(2,1)S(1)}, u32[]{:S(2)}) %copy-start.1) | copy-done | bytes 1048600
  46.2 3.0 %all-to-all-done.1.kv_ref.far_ref = bf16[8,2,128,128]{3,2,1,0:T(8,128)(2,1)S(1)} async-done(((bf16[8,2,128,128]{3,2,1,0:T(8,128)(2,1)}), bf16[8,2,128,128]{3,2,1,0:T(8,128)(2,1)S(1)}, u32[]{:S(2)}, u32[]{:S(2)}) %all-to-all-start.1) | async-done | bytes 524320 | tf_op jit(solution)/shard_map/all_to_all | solution.py:254
  49.2 1.9 %far.1 = (bf16[8,128,512]{2,1,0:T(8,128)(2,1)S(1)}, f32[128,512]{1,0:T(8,128)S(1)}, f32[8,512]{1,0:T(8,128)S(1)}, f32[2,128]{1,0:T(2,128)S(1)}) custom-call(s32[2]{0:T(128)S(1)} %pad_add_fusion.place, s32[1,16]{1,0:T(1,128)S(1)} %copy-done.4, bf16[128,512]{1,0:T(8,128)(2,1)S(1)} %copy-done, bf16[8,2,128,128]{3,2,1,0:T(8,128)(2,1)S(1)} %all-to-all-done.1.kv_ref.far_ref, ...), custom_call_target="tpu_custom_call" | custom-call | flops 280000000 | bytes 3000000 | tf_op jit(solution)/shard_map/far/pallas_call | solution.py:261
  51.2 9.4 %all_to_all.25.sums_ref = f32[8,2,128]{2,1,0:T(2,128)S(1)} all-to-all(f32[8,2,128]{2,1,0:T(2,128)S(1)} %broadcast_in_dim.79), channel_id=1, replica_groups=mesh['zq'=16,'zp'=2,'y'=4,'head'=8] {'head'}, dimensions={0} | all-to-all | bytes 16384 | tf_op jit(solution)/shard_map/all_to_all | solution.py:264
  60.6 2.6 %far_back.1 = (bf16[8,2,128,128]{3,2,1,0:T(8,128)(2,1)}, bf16[128,512]{1,0:T(8,128)(2,1)S(1)}, f32[8,512]{1,0:T(8,128)S(1)}, f32[8,128]{1,0:T(8,128)S(1)}) custom-call(bf16[128,512]{1,0:T(8,128)(2,1)S(1)} %copy-done, bf16[8,2,128,128]{3,2,1,0:T(8,128)(2,1)S(1)} %all-to-all-done.1.kv_ref.far_ref, bf16[8,128,512]{2,1,0:T(8,128)(2,1)S(1)} %get-tuple-element.27.w_ref.w_far_ref, ...), custom_call_target="tpu_custom_call" | custom-call | flops 400000000 | bytes 4000000 | tf_op jit(solution)/shard_map/far_back/pallas_call | solution.py:265
  63.2 5.1 %all-to-all-start.4 = ((bf16[8,2,128,128]{3,2,1,0:T(8,128)(2,1)}), bf16[8,2,128,128]{3,2,1,0:T(8,128)(2,1)S(1)}, u32[]{:S(2)}, u32[]{:S(2)}) async-start(bf16[8,2,128,128]{3,2,1,0:T(8,128)(2,1)} %get-tuple-element.37), calls=%async_computation.4 | async-start | bytes 1048576 | tf_op jit(solution)/shard_map/all_to_all | solution.py:271
  68.3 1.2 %copy-done.2 = bf16[8,128,512]{2,1,0:T(8,128)(2,1)S(1)} copy-done((bf16[8,128,512]{2,1,0:T(8,128)(2,1)S(1)}, bf16[8,128,512]{2,1,0:T(8,128)(2,1)}, u32[]{:S(2)}) %copy-start.2) | copy-done | bytes 1048600
  69.5 4.6 %near_back.1 = (bf16[8,2,128,128]{3,2,1,0:T(8,128)(2,1)}, bf16[128,512]{1,0:T(8,128)(2,1)}, bf16[128,512]{1,0:T(8,128)(2,1)}) custom-call(bf16[128,512]{1,0:T(8,128)(2,1)S(1)} %copy-done, bf16[8,2,128,128]{3,2,1,0:T(8,128)(2,1)S(1)} %all-to-all-done.kv_ref.near_ref, bf16[8,2,128,128]{3,2,1,0:T(8,128)(2,1)S(1)} %all-to-all-done.1.kv_ref.far_ref, ...), custom_call_target="tpu_custom_call" | custom-call | flops 800000000 | bytes 6000000 | tf_op jit(solution)/shard_map/near_back/pallas_call | solution.py:273
  74.1 2.4 %all-to-all-done.4.far_ref = bf16[8,2,128,128]{3,2,1,0:T(8,128)(2,1)S(1)} async-done(((bf16[8,2,128,128]{3,2,1,0:T(8,128)(2,1)}), bf16[8,2,128,128]{3,2,1,0:T(8,128)(2,1)S(1)}, u32[]{:S(2)}, u32[]{:S(2)}) %all-to-all-start.4) | async-done | bytes 524320 | tf_op jit(solution)/shard_map/all_to_all | solution.py:271
  76.5 4.8 %all-to-all-start.3 = ((bf16[8,2,128,128]{3,2,1,0:T(8,128)(2,1)}), bf16[8,2,128,128]{3,2,1,0:T(8,128)(2,1)S(1)}, u32[]{:S(2)}, u32[]{:S(2)}) async-start(bf16[8,2,128,128]{3,2,1,0:T(8,128)(2,1)} %get-tuple-element.36), calls=%async_computation.3 | async-start | bytes 1048576 | tf_op jit(solution)/shard_map/all_to_all | solution.py:276
  81.4 0.8 sums.1
  82.1 1.9 %collective-permute-start.2 = (bf16[2,128,128]{2,1,0:T(8,128)(2,1)S(1)}, bf16[2,128,128]{2,1,0:T(8,128)(2,1)S(1)}, u32[]{:S(2)}, u32[]{:S(2)}) collective-permute-start(bf16[2,128,128]{2,1,0:T(8,128)(2,1)S(1)} %get-tuple-element.38), channel_id=1, source_target_pairs={{0,64},{64,128},{128,192},{192,256},{256,320},{320,384},{384,448},... | collective-permute-start | bytes 196616 | tf_op jit(solution)/shard_map/ppermute | solution.py:218
  84.0 6.0 %collective-permute-start.3 = (bf16[2,128,128]{2,1,0:T(8,128)(2,1)S(1)}, bf16[2,128,128]{2,1,0:T(8,128)(2,1)S(1)}, u32[]{:S(2)}, u32[]{:S(2)}) collective-permute-start(bf16[2,128,128]{2,1,0:T(8,128)(2,1)S(1)} %get-tuple-element.39), channel_id=1, source_target_pairs={{0,960},{64,0},{128,64},{192,128},{256,192},{320,256},{384,320},{4... | collective-permute-start | bytes 196616 | tf_op jit(solution)/shard_map/ppermute | solution.py:218
  90.7 1.6 %collective-permute-done.3.above_ref = bf16[2,128,128]{2,1,0:T(8,128)(2,1)S(1)} collective-permute-done((bf16[2,128,128]{2,1,0:T(8,128)(2,1)S(1)}, bf16[2,128,128]{2,1,0:T(8,128)(2,1)S(1)}, u32[]{:S(2)}, u32[]{:S(2)}) %collective-permute-start.3) | collective-permute-done | bytes 65568 | tf_op jit(solution)/shard_map/ppermute | solution.py:218
  92.3 0.7 last.1
  (18 shorter events, 1.3 us)
Async XLA Ops:
  2.4 34.3 %all-to-all-start = ((bf16[8,2,128,128]{3,2,1,0:T(8,128)(2,1)}), bf16[8,2,128,128]{3,2,1,0:T(8,128)(2,1)S(1)}, u32[]{:S(2)}, u32[]{:S(2)}) async-start(bf16[8,2,128,128]{3,2,1,0:T(8,128)(2,1)} %broadcast_in_dim.74), calls=%async_computation | async-start | bytes 1048576 | tf_op jit(solution)/shard_map/all_to_all | solution.py:250
  18.9 9.9 %collective-permute-start.1 = (bf16[2,128,128]{2,1,0:T(8,128)(2,1)S(1)}, bf16[2,128,128]{2,1,0:T(8,128)(2,1)S(1)}, u32[]{:S(2)}, u32[]{:S(2)}) collective-permute-start(bf16[2,128,128]{2,1,0:T(8,128)(2,1)S(1)} %broadcast_select_fusion.1), channel_id=1, source_target_pairs={{0,960},{64,0},{128,64},{192,128},{256,192},{320,256},{384,320},{4... | collective-permute-start | bytes 196616 | tf_op jit(solution)/shard_map/ppermute | solution.py:218
  26.9 8.9 %collective-permute-start = (bf16[2,128,128]{2,1,0:T(8,128)(2,1)S(1)}, bf16[2,128,128]{2,1,0:T(8,128)(2,1)S(1)}, u32[]{:S(2)}, u32[]{:S(2)}) collective-permute-start(bf16[2,128,128]{2,1,0:T(8,128)(2,1)S(1)} %broadcast_select_fusion.1), channel_id=1, source_target_pairs={{0,64},{64,128},{128,192},{192,256},{256,320},{320,384},{384,448},... | collective-permute-start | bytes 196616 | tf_op jit(solution)/shard_map/ppermute | solution.py:218
  36.7 6.0 %copy-start = (bf16[128,512]{1,0:T(8,128)(2,1)S(1)}, bf16[128,512]{1,0:T(8,128)(2,1)}, u32[]{:S(2)}) copy-start(bf16[128,512]{1,0:T(8,128)(2,1)} %q_ref.7) | copy-start | bytes 393220
  36.7 6.0 %copy-start.5 = (bf16[128,512]{1,0:T(8,128)(2,1)S(1)}, bf16[128,512]{1,0:T(8,128)(2,1)}, u32[]{:S(2)}) copy-start(bf16[128,512]{1,0:T(8,128)(2,1)} %up_ref.1) | copy-start | bytes 393220
  36.7 12.5 %all-to-all-start.1 = ((bf16[8,2,128,128]{3,2,1,0:T(8,128)(2,1)}), bf16[8,2,128,128]{3,2,1,0:T(8,128)(2,1)S(1)}, u32[]{:S(2)}, u32[]{:S(2)}) async-start(bf16[8,2,128,128]{3,2,1,0:T(8,128)(2,1)} %broadcast_select_fusion), calls=%async_computation.1 | async-start | bytes 1048576 | tf_op jit(solution)/shard_map/all_to_all | solution.py:254
  42.6 0.7 copy-start.3
  42.7 0.7 copy-start.4
  45.2 1.0 %copy-start.1 = (bf16[8,128,512]{2,1,0:T(8,128)(2,1)}, bf16[8,128,512]{2,1,0:T(8,128)(2,1)S(1)}, u32[]{:S(2)}) copy-start(bf16[8,128,512]{2,1,0:T(8,128)(2,1)S(1)} %get-tuple-element.23.w_near_ref) | copy-start | bytes 3145732
  63.2 13.4 %all-to-all-start.4 = ((bf16[8,2,128,128]{3,2,1,0:T(8,128)(2,1)}), bf16[8,2,128,128]{3,2,1,0:T(8,128)(2,1)S(1)}, u32[]{:S(2)}, u32[]{:S(2)}) async-start(bf16[8,2,128,128]{3,2,1,0:T(8,128)(2,1)} %get-tuple-element.37), calls=%async_computation.4 | async-start | bytes 1048576 | tf_op jit(solution)/shard_map/all_to_all | solution.py:271
  68.2 1.2 %copy-start.2 = (bf16[8,128,512]{2,1,0:T(8,128)(2,1)S(1)}, bf16[8,128,512]{2,1,0:T(8,128)(2,1)}, u32[]{:S(2)}) copy-start(bf16[8,128,512]{2,1,0:T(8,128)(2,1)} %copy-done.1) | copy-start | bytes 3145732
  76.5 13.6 %all-to-all-start.3 = ((bf16[8,2,128,128]{3,2,1,0:T(8,128)(2,1)}), bf16[8,2,128,128]{3,2,1,0:T(8,128)(2,1)S(1)}, u32[]{:S(2)}, u32[]{:S(2)}) async-start(bf16[8,2,128,128]{3,2,1,0:T(8,128)(2,1)} %get-tuple-element.36), calls=%async_computation.3 | async-start | bytes 1048576 | tf_op jit(solution)/shard_map/all_to_all | solution.py:276
  82.1 8.5 %collective-permute-start.2 = (bf16[2,128,128]{2,1,0:T(8,128)(2,1)S(1)}, bf16[2,128,128]{2,1,0:T(8,128)(2,1)S(1)}, u32[]{:S(2)}, u32[]{:S(2)}) collective-permute-start(bf16[2,128,128]{2,1,0:T(8,128)(2,1)S(1)} %get-tuple-element.38), channel_id=1, source_target_pairs={{0,64},{64,128},{128,192},{192,256},{256,320},{320,384},{384,448},... | collective-permute-start | bytes 196616 | tf_op jit(solution)/shard_map/ppermute | solution.py:218
  84.0 8.2 %collective-permute-start.3 = (bf16[2,128,128]{2,1,0:T(8,128)(2,1)S(1)}, bf16[2,128,128]{2,1,0:T(8,128)(2,1)S(1)}, u32[]{:S(2)}, u32[]{:S(2)}) collective-permute-start(bf16[2,128,128]{2,1,0:T(8,128)(2,1)S(1)} %get-tuple-element.39), channel_id=1, source_target_pairs={{0,960},{64,0},{128,64},{192,128},{256,192},{320,256},{384,320},{4... | collective-permute-start | bytes 196616 | tf_op jit(solution)/shard_map/ppermute | solution.py:218

commit v3 on v1

v3 whole, which is shorter than its diff:
```python
import math

import jax
import jax.numpy as jnp
from jax import lax
from jax.experimental import pallas as pl
from jax.experimental.pallas import tpu as pltpu
from jax.sharding import Mesh
from jax.sharding import PartitionSpec as P

HEADS = 32
KV_HEADS = 8
GROUP = HEADS // KV_HEADS
DH = 128
BLK = 128
ROWS = GROUP * BLK
PEERS = 8
NEGATIVE = -1e30
EPSILON = 1e-06
FEATURES = HEADS * DH
SCALING = DH ** (-0.5)
EXP2_SCALE = SCALING / math.log(2.0)
PAIR = ("zp", "y")
VMEM_LIMIT = 12 * 1024 * 1024


def window_slot(zp, y, peer, part):
    peer_zp, peer_y = peer // 4, peer % 4
    across = (zp - peer_zp) & 1
    shift = peer_y - y
    if part == 0:
        return 8 + shift + across * (4 * (1 - 2 * zp))
    same = shift & 15
    other = 8 + shift - 4 * (1 - 2 * zp)
    return jnp.where(across == 1, other, same)


def stacked(array):
    return jnp.concatenate([array[:, g * DH : (g + 1) * DH] for g in range(GROUP)], axis=0)


def stacked_t(array):
    return jnp.concatenate([array[:, g * DH : (g + 1) * DH].T for g in range(GROUP)], axis=1)


def unstacked_t(array):
    return jnp.concatenate([array[:, g * BLK : (g + 1) * BLK].T for g in range(GROUP)], axis=1)


def over_groups(row):
    return sum(row[:, g * BLK : (g + 1) * BLK] for g in range(GROUP))


def to_groups(row):
    return jnp.concatenate([row] * GROUP, axis=1)


def forward_kernel(mask, q_ref, kv_ref, up_ref, gain_ref, w_ref, att_ref, up_out, inv_ref, part_ref, s_ref):
    zp, y = lax.axis_index("zp"), lax.axis_index("y")
    q_t = stacked_t(q_ref[...])
    top = jnp.full((8, ROWS), NEGATIVE, jnp.float32)
    for slot in range(2 * PEERS):
        peer, part = slot // 2, slot % 2
        bias = jnp.where(mask[0, window_slot(zp, y, peer, part)] > 0, 0.0, NEGATIVE)
        raw = jnp.dot(kv_ref[peer, part, 0], q_t, preferred_element_type=jnp.float32) + bias
        s_ref[slot] = raw
        top = jnp.maximum(top, raw.reshape(BLK // 8, 8, ROWS).max(axis=0))
    top = top.max(axis=0, keepdims=True)
    total = jnp.zeros((8, ROWS), jnp.float32)
    numer = jnp.zeros((DH, ROWS), jnp.float32)
    for slot in range(2 * PEERS):
        weights = jnp.exp2((s_ref[slot] - top) * EXP2_SCALE)
        total = total + weights.reshape(BLK // 8, 8, ROWS).sum(axis=0)
        rounded = weights.astype(jnp.bfloat16)
        w_ref[slot // 2, slot % 2] = rounded
        values_t = kv_ref[slot // 2, slot % 2, 1].T
        numer = numer + jnp.dot(values_t, rounded, preferred_element_type=jnp.float32)
    inverse = 1.0 / total.sum(axis=0, keepdims=True)
    attended = numer * inverse
    att_ref[...] = attended
    inv_ref[...] = jnp.broadcast_to(inverse, (8, ROWS))
    upstream = stacked_t(up_ref[...].astype(jnp.float32) * gain_ref[...])
    up_out[...] = upstream
    squares = over_groups(jnp.sum(attended * attended, axis=0, keepdims=True))
    products = over_groups(jnp.sum(upstream * attended, axis=0, keepdims=True))
    part_ref[...] = jnp.concatenate([squares, products], axis=0)


def rows_of(do_t):
    return jnp.concatenate([do_t[:, g * BLK : (g + 1) * BLK].T for g in range(GROUP)], axis=0)


def backward_kernel(q_ref, kv_ref, w_ref, att_ref, up_ref, inv_ref, sums_ref, terms_ref, grad_ref, normed_ref):
    sums = sums_ref[0]
    for peer in range(1, KV_HEADS):
        sums = sums + sums_ref[peer]
    root = jnp.sqrt(sums[0:1] / FEATURES + EPSILON)
    inv_root = 1.0 / root
    inner = sums[1:2] * inv_root
    attended = att_ref[...]
    normed = attended * to_groups(inv_root)
    normed_ref[...] = normed
    d_att = (up_ref[...] - normed * to_groups(inner / FEATURES)) * to_groups(inv_root)
    d_att = d_att.astype(jnp.bfloat16).astype(jnp.float32)
    inverse = inv_ref[0:1]
    delta = jnp.sum(d_att * attended, axis=0, keepdims=True) * inverse
    do_t = (d_att * inverse).astype(jnp.bfloat16)
    do_rows = rows_of(do_t)
    q_rows = stacked(q_ref[...])
    grad = jnp.zeros((DH, ROWS), jnp.float32)
    for slot in range(2 * PEERS):
        peer, part = slot // 2, slot % 2
        weights = w_ref[peer, part]
        d_prob = jnp.dot(kv_ref[peer, part, 1], do_t, preferred_element_type=jnp.float32)
        d_score = (weights.astype(jnp.float32) * (d_prob - delta)).astype(jnp.bfloat16)
        term_k = jnp.dot(d_score, q_rows, preferred_element_type=jnp.float32) * SCALING
        term_v = jnp.dot(weights, do_rows, preferred_element_type=jnp.float32)
        terms_ref[peer, part, 0] = term_k.astype(jnp.bfloat16)
        terms_ref[peer, part, 1] = term_v.astype(jnp.bfloat16)
        grad = grad + jnp.dot(kv_ref[peer, part, 0].T, d_score, preferred_element_type=jnp.float32)
    grad_ref[...] = grad


def far_sums_kernel(terms_ref, below_ref, above_ref):
    zp, y = lax.axis_index("zp"), lax.axis_index("y")
    below = jnp.zeros((2, BLK, DH), jnp.float32)
    above = jnp.zeros((2, BLK, DH), jnp.float32)
    for peer in range(PEERS):
        take = jnp.where(zp == peer // 4, y >= peer % 4, zp == 1)
        share = jnp.where(take, 1.0, 0.0)
        term = terms_ref[peer, 1].astype(jnp.float32)
        below = below + term * share
        above = above + term * (1.0 - share)
    below_ref[...] = below.astype(jnp.bfloat16)
    above_ref[...] = above.astype(jnp.bfloat16)


def near_sums_kernel(terms_ref, grad_ref, normed_ref, gain_ref, sum_ref, grad_out, out_ref):
    total = jnp.zeros((2, BLK, DH), jnp.float32)
    for peer in range(PEERS):
        total = total + terms_ref[peer, 0].astype(jnp.float32)
    sum_ref[...] = total
    grad_out[...] = (unstacked_t(grad_ref[...]) * SCALING).astype(jnp.bfloat16)
    out_ref[...] = (unstacked_t(normed_ref[...]) * gain_ref[...]).astype(jnp.bfloat16)


def last_kernel(near_ref, below_ref, above_ref, keys_ref, values_ref):
    total = near_ref[...] + below_ref[...].astype(jnp.float32) + above_ref[...].astype(jnp.float32)
    keys_ref[...] = total[0].astype(jnp.bfloat16)
    values_ref[...] = total[1].astype(jnp.bfloat16)


def shape(dims, dtype):
    return jax.ShapeDtypeStruct(dims, dtype)


def in_vmem(count):
    return [pl.BlockSpec(memory_space=pltpu.VMEM)] * count


def in_smem(count):
    return [pl.BlockSpec(memory_space=pltpu.SMEM)] * count


def two_planes(array, by):
    length = lax.axis_size("zq")
    return lax.ppermute(array, "zq", [(i, (i + by) % length) for i in range(length)])


def call(kernel, name, outs, smem, vmem, scratch=(), flops=0, size=0):
    specs = tuple(in_vmem(len(outs)))
    return pl.pallas_call(
        kernel,
        out_shape=tuple(outs),
        in_specs=in_smem(smem) + in_vmem(vmem),
        out_specs=specs,
        scratch_shapes=list(scratch),
        compiler_params=pltpu.CompilerParams(vmem_limit_bytes=VMEM_LIMIT),
        cost_estimate=pl.CostEstimate(flops=flops, bytes_accessed=size, transcendentals=0),
        name=name,
    )


def per_device(queries, keys_in, values_in, norm_gain, grad_out, nearby_block_mask):
    zp, y = lax.axis_index("zp"), lax.axis_index("y")
    gain = norm_gain.reshape(1, -1)
    bf16, f32 = jnp.bfloat16, jnp.float32
    block = (2, BLK, DH)
    columns = shape((DH, ROWS), f32)
    row = shape((8, ROWS), f32)

    first = jnp.arange(2, dtype=jnp.int32)[:, None, None] == 0
    own = jnp.where(first, keys_in[None], values_in[None])
    above = two_planes(own, -1)
    below = two_planes(own, 1)
    index = jnp.arange(2 * PEERS, dtype=jnp.int32).reshape(PEERS, 2, 1, 1, 1)
    to_zp, to_y = index // 8, index // 2 % 4
    take_below = jnp.where(to_zp == zp, y >= to_y, zp == 1)
    chosen = jnp.where(take_below, below[None, None], above[None, None])
    gathered = lax.all_to_all(jnp.where(index % 2 == 0, own[None, None], chosen), PAIR, 0, 0)

    scores = [pltpu.VMEM((2 * PEERS, BLK, ROWS), f32)]
    weights, attended, upstream, inverse, part = call(
        forward_kernel,
        "forward",
        (shape((PEERS, 2, BLK, ROWS), bf16), columns, columns, row, shape((2, BLK), f32)),
        1, 4, scores, 550_000_000, 5_000_000,
    )(nearby_block_mask, queries, gathered, grad_out, gain)
    sums = lax.all_to_all(jnp.broadcast_to(part[None], (KV_HEADS, 2, BLK)), "head", 0, 0)
    terms, grad_t, normed_t = call(
        backward_kernel,
        "backward",
        (shape((PEERS, 2) + block, bf16), columns, columns),
        0, 7, (), 1_100_000_000, 5_000_000,
    )(queries, gathered, weights, attended, upstream, inverse, sums)
    returned = lax.all_to_all(terms, PAIR, 0, 0)
    half = shape(block, bf16)
    to_below, to_above = call(far_sums_kernel, "far_sums", (half, half), 0, 1, (), 1_000_000, 600_000)(returned)
    from_above = two_planes(to_below, -1)
    from_below = two_planes(to_above, 1)
    tall = shape((BLK, GROUP * DH), bf16)
    near_sum, grad_queries, normed_out = call(
        near_sums_kernel, "near_sums", (shape(block, f32), tall, tall), 0, 4, (), 1_000_000, 1_500_000
    )(returned, grad_t, normed_t, gain)
    piece = shape((BLK, DH), bf16)
    grad_keys, grad_values = call(last_kernel, "last", (piece, piece), 0, 3, (), 1_000_000, 300_000)(
        near_sum, from_below, from_above
    )
    return normed_out, grad_queries, grad_keys, grad_values


def solution(mesh):
    spans, heads = mesh.devices.shape
    fine = Mesh(mesh.devices.reshape(spans // 8, 2, 4, heads), ("zq", "zp", "y", "head"))
    seq = ("zq", "zp", "y")
    both = P(seq, "head")
    return jax.shard_map(
        per_device,
        mesh=fine,
        in_specs=(both, both, both, P("head"), both, P(seq, None)),
        out_specs=(both, both, both, both),
        check_vma=False,
    )
```

time: 99 us -> 94.4 us (0.954)
  the two profiles are of different devices: /device:TPU:32 before, /device:TPU:2 now
where the time goes in v3:
time: 94.4 us; the launch traced here: 94.1 us
  blocking collectives  46.3 us (49%)
  starting transfers between devices  29 us (31%)
  Pallas kernels  8.74 us (9%)
  waiting for transfers between devices  8.1 us (9%)
  other arithmetic  1.19 us (1%)
    ppermute x4, starting transfers between devices, two_planes(): lax.ppermute(array, 'zq', [(i, (i + by) % length) for i in range(length)])  29 us
    all_to_all x1, blocking collectives, per_device(): lax.all_to_all(jnp.where(index % 2 == 0, own[None, None], chosen), PAIR,...  19.4 us
    all_to_all x1, blocking collectives, per_device(): returned = lax.all_to_all(terms, PAIR, 0, 0)  18.5 us
    all_to_all x1, blocking collectives, per_device(): lax.all_to_all(jnp.broadcast_to(part[None], (KV_HEADS, 2, BLK)), 'head',...  8.48 us
    ppermute x4, waiting for transfers between devices, two_planes(): lax.ppermute(array, 'zq', [(i, (i + by) % length) for i in range(length)])  8.1 us
    pallas_call x1, Pallas kernels, per_device(): call(backward_kernel, 'backward', (shape((PEERS, 2) + block, bf16), colum...  4.13 us
    pallas_call x1, Pallas kernels, per_device(): call(forward_kernel, 'forward', (shape((PEERS, 2, BLK, ROWS), bf16), colu...  2.87 us
  transfers between devices with their start and end apart: 4, of which 3 were waited for; matrix products, arithmetic and copies ran while one was open for 0% of the time, Pallas kernels for 1%

profile of v3, /device:TPU:2, one launch (start us, length us, event | category | flops | bytes accessed | tf_op | source)
XLA Modules:
  0.0 94.1 jit_solution(2023523728777140202)
XLA Ops:
  0.6 0.0 copy-start.2
  0.6 0.0 copy-start.3
  0.7 0.0 copy-start.1
  0.7 0.0 copy-start
  0.7 1.0 %broadcast_select_fusion = bf16[2,128,128]{2,1,0:T(8,128)(2,1)S(1)} fusion(pred[2]{0:T(512)(128)(4,1)S(1)} %iota_compare_fusion, bf16[128,128]{1,0:T(8,128)(2,1)} %param.8, bf16[128,128]{1,0:T(8,128)(2,1)} %param.7), kind=kLoop, calls=%fused_computation.1 | loop fusion | flops 32768 | bytes 131074 | tf_op jit(solution)/shard_map/jit(_where)/select_n | solution.py:193
  1.6 19.1 %collective-permute-start.1 = (bf16[2,128,128]{2,1,0:T(8,128)(2,1)S(1)}, bf16[2,128,128]{2,1,0:T(8,128)(2,1)S(1)}, u32[]{:S(2)}, u32[]{:S(2)}) collective-permute-start(bf16[2,128,128]{2,1,0:T(8,128)(2,1)S(1)} %broadcast_select_fusion), channel_id=1, source_target_pairs={{0,960},{64,0},{128,64},{192,128},{256,192},{320,256},{384,320},{4... | collective-permute-start | bytes 196616 | tf_op jit(solution)/shard_map/ppermute | solution.py:167
  20.8 1.9 %collective-permute-start = (bf16[2,128,128]{2,1,0:T(8,128)(2,1)S(1)}, bf16[2,128,128]{2,1,0:T(8,128)(2,1)S(1)}, u32[]{:S(2)}, u32[]{:S(2)}) collective-permute-start(bf16[2,128,128]{2,1,0:T(8,128)(2,1)S(1)} %broadcast_select_fusion), channel_id=1, source_target_pairs={{0,64},{64,128},{128,192},{192,256},{256,320},{320,384},{384,448},... | collective-permute-start | bytes 196616 | tf_op jit(solution)/shard_map/ppermute | solution.py:167
  22.7 0.8 collective-permute-done.1
  23.5 5.7 %collective-permute-done = bf16[2,128,128]{2,1,0:T(8,128)(2,1)S(1)} collective-permute-done((bf16[2,128,128]{2,1,0:T(8,128)(2,1)S(1)}, bf16[2,128,128]{2,1,0:T(8,128)(2,1)S(1)}, u32[]{:S(2)}, u32[]{:S(2)}) %collective-permute-start) | collective-permute-done | bytes 65568 | tf_op jit(solution)/shard_map/ppermute | solution.py:167
  29.2 0.2 select_select_fusion
  29.4 19.4 %all_to_all.15.kv_ref = bf16[8,2,2,128,128]{4,3,2,1,0:T(8,128)(2,1)S(1)} all-to-all(bf16[8,2,2,128,128]{4,3,2,1,0:T(8,128)(2,1)S(1)} %select_select_fusion), channel_id=1, replica_groups=mesh['zq'=16,'zp'=2,'y'=4,'head'=8] {'zp','y'}, dimensions={0} | all-to-all | bytes 2097152 | tf_op jit(solution)/shard_map/all_to_all | solution.py:200
  48.8 0.0 copy-done.2
  48.8 0.0 copy-done.3
  48.8 2.9 %forward.1 = (bf16[8,2,128,512]{3,2,1,0:T(8,128)(2,1)S(1)}, f32[128,512]{1,0:T(8,128)S(1)}, f32[128,512]{1,0:T(8,128)S(1)}, f32[8,512]{1,0:T(8,128)S(1)}, f32[2,128]{1,0:T(2,128)S(1)}) custom-call(s32[1,16]{1,0:T(1,128)S(1)} %copy-done.3, bf16[128,512]{1,0:T(8,128)(2,1)S(1)} %copy-done.2, bf16[8,2,2,128,128]{4,3,2,1,0:T(8,128)(2,1)S(1)} %all_to_all.15.kv_ref, ...), custom_call_target="tpu_custom_call" | custom-call | flops 550000000 | bytes 5000000 | tf_op jit(solution)/shard_map/forward/pallas_call | solution.py:203
  51.7 8.5 %all_to_all.16.sums_ref = f32[8,2,128]{2,1,0:T(2,128)S(1)} all-to-all(f32[8,2,128]{2,1,0:T(2,128)S(1)} %broadcast_in_dim.89), channel_id=1, replica_groups=mesh['zq'=16,'zp'=2,'y'=4,'head'=8] {'head'}, dimensions={0} | all-to-all | bytes 16384 | tf_op jit(solution)/shard_map/all_to_all | solution.py:209
  60.2 4.1 %backward.1 = (bf16[8,2,2,128,128]{4,3,2,1,0:T(8,128)(2,1)S(1)}, f32[128,512]{1,0:T(8,128)S(1)}, f32[128,512]{1,0:T(8,128)S(1)}) custom-call(bf16[128,512]{1,0:T(8,128)(2,1)S(1)} %copy-done.2, bf16[8,2,2,128,128]{4,3,2,1,0:T(8,128)(2,1)S(1)} %all_to_all.15.kv_ref, bf16[8,2,128,512]{3,2,1,0:T(8,128)(2,1)S(1)} %get-tuple-element.19.w_ref, ...), custom_call_target="tpu_custom_call" | custom-call | flops 1100000000 | bytes 5000000 | tf_op jit(solution)/shard_map/backward/pallas_call | solution.py:210
  64.3 18.5 %all_to_all.17.terms_ref = bf16[8,2,2,128,128]{4,3,2,1,0:T(8,128)(2,1)S(1)} all-to-all(bf16[8,2,2,128,128]{4,3,2,1,0:T(8,128)(2,1)S(1)} %get-tuple-element.24), channel_id=1, replica_groups=mesh['zq'=16,'zp'=2,'y'=4,'head'=8] {'zp','y'}, dimensions={0} | all-to-all | bytes 2097152 | tf_op jit(solution)/shard_map/all_to_all | solution.py:216
  82.8 0.2 far_sums.1
  83.0 1.9 %collective-permute-start.2 = (bf16[2,128,128]{2,1,0:T(8,128)(2,1)S(1)}, bf16[2,128,128]{2,1,0:T(8,128)(2,1)S(1)}, u32[]{:S(2)}, u32[]{:S(2)}) collective-permute-start(bf16[2,128,128]{2,1,0:T(8,128)(2,1)S(1)} %get-tuple-element.30), channel_id=1, source_target_pairs={{0,64},{64,128},{128,192},{192,256},{256,320},{320,384},{384,448},... | collective-permute-start | bytes 196616 | tf_op jit(solution)/shard_map/ppermute | solution.py:167
  84.9 6.0 %collective-permute-start.3 = (bf16[2,128,128]{2,1,0:T(8,128)(2,1)S(1)}, bf16[2,128,128]{2,1,0:T(8,128)(2,1)S(1)}, u32[]{:S(2)}, u32[]{:S(2)}) collective-permute-start(bf16[2,128,128]{2,1,0:T(8,128)(2,1)S(1)} %get-tuple-element.31), channel_id=1, source_target_pairs={{0,960},{64,0},{128,64},{192,128},{256,192},{320,256},{384,320},{4... | collective-permute-start | bytes 196616 | tf_op jit(solution)/shard_map/ppermute | solution.py:167
  91.0 0.9 near_sums.1
  91.8 0.0 collective-permute-done.2.below_ref
  91.8 1.6 %collective-permute-done.3.above_ref = bf16[2,128,128]{2,1,0:T(8,128)(2,1)S(1)} collective-permute-done((bf16[2,128,128]{2,1,0:T(8,128)(2,1)S(1)}, bf16[2,128,128]{2,1,0:T(8,128)(2,1)S(1)}, u32[]{:S(2)}, u32[]{:S(2)}) %collective-permute-start.3) | collective-permute-done | bytes 65568 | tf_op jit(solution)/shard_map/ppermute | solution.py:167
  93.5 0.6 last.1
  (5 shorter events, 0.0 us)
Async XLA Ops:
  0.6 48.2 %copy-start.2 = (bf16[128,512]{1,0:T(8,128)(2,1)S(1)}, bf16[128,512]{1,0:T(8,128)(2,1)}, u32[]{:S(2)}) copy-start(bf16[128,512]{1,0:T(8,128)(2,1)} %q_ref.3) | copy-start | bytes 393220
  0.6 48.1 %copy-start.3 = (s32[1,16]{1,0:T(1,128)S(1)}, s32[1,16]{1,0:T(1,128)}, u32[]{:S(2)}) copy-start(s32[1,16]{1,0:T(1,128)} %mask.1) | copy-start | bytes 196
  0.7 48.1 %copy-start.1 = (bf16[128,512]{1,0:T(8,128)(2,1)S(1)}, bf16[128,512]{1,0:T(8,128)(2,1)}, u32[]{:S(2)}) copy-start(bf16[128,512]{1,0:T(8,128)(2,1)} %up_ref.1) | copy-start | bytes 393220
  0.7 48.1 %copy-start = (f32[512]{0:T(512)S(1)}, f32[512]{0:T(512)}, u32[]{:S(2)}) copy-start(f32[512]{0:T(512)} %param.9) | copy-start | bytes 6148
  1.6 21.9 %collective-permute-start.1 = (bf16[2,128,128]{2,1,0:T(8,128)(2,1)S(1)}, bf16[2,128,128]{2,1,0:T(8,128)(2,1)S(1)}, u32[]{:S(2)}, u32[]{:S(2)}) collective-permute-start(bf16[2,128,128]{2,1,0:T(8,128)(2,1)S(1)} %broadcast_select_fusion), channel_id=1, source_target_pairs={{0,960},{64,0},{128,64},{192,128},{256,192},{320,256},{384,320},{4... | collective-permute-start | bytes 196616 | tf_op jit(solution)/shard_map/ppermute | solution.py:167
  20.8 8.4 %collective-permute-start = (bf16[2,128,128]{2,1,0:T(8,128)(2,1)S(1)}, bf16[2,128,128]{2,1,0:T(8,128)(2,1)S(1)}, u32[]{:S(2)}, u32[]{:S(2)}) collective-permute-start(bf16[2,128,128]{2,1,0:T(8,128)(2,1)S(1)} %broadcast_select_fusion), channel_id=1, source_target_pairs={{0,64},{64,128},{128,192},{192,256},{256,320},{320,384},{384,448},... | collective-permute-start | bytes 196616 | tf_op jit(solution)/shard_map/ppermute | solution.py:167
  83.0 8.8 %collective-permute-start.2 = (bf16[2,128,128]{2,1,0:T(8,128)(2,1)S(1)}, bf16[2,128,128]{2,1,0:T(8,128)(2,1)S(1)}, u32[]{:S(2)}, u32[]{:S(2)}) collective-permute-start(bf16[2,128,128]{2,1,0:T(8,128)(2,1)S(1)} %get-tuple-element.30), channel_id=1, source_target_pairs={{0,64},{64,128},{128,192},{192,256},{256,320},{320,384},{384,448},... | collective-permute-start | bytes 196616 | tf_op jit(solution)/shard_map/ppermute | solution.py:167
  84.9 8.5 %collective-permute-start.3 = (bf16[2,128,128]{2,1,0:T(8,128)(2,1)S(1)}, bf16[2,128,128]{2,1,0:T(8,128)(2,1)S(1)}, u32[]{:S(2)}, u32[]{:S(2)}) collective-permute-start(bf16[2,128,128]{2,1,0:T(8,128)(2,1)S(1)} %get-tuple-element.31), channel_id=1, source_target_pairs={{0,960},{64,0},{128,64},{192,128},{256,192},{320,256},{384,320},{4... | collective-permute-start | bytes 196616 | tf_op jit(solution)/shard_map/ppermute | solution.py:167

commit v4 on v3

--- a/solution.py
+++ b/solution.py
@@ -15,6 +15,8 @@
 BLK = 128
 ROWS = GROUP * BLK
 PEERS = 8
+FORWARD_STEP = 2
+BACKWARD_STEP = 4
 NEGATIVE = -1e30
 EPSILON = 1e-06
 FEATURES = HEADS * DH
@@ -55,25 +57,32 @@
     return jnp.concatenate([row] * GROUP, axis=1)
 
 
+def joined(ref, first, count, which):
+    return jnp.concatenate([ref[slot // 2, slot % 2, which] for slot in range(first, first + count)], axis=0)
+
+
 def forward_kernel(mask, q_ref, kv_ref, up_ref, gain_ref, w_ref, att_ref, up_out, inv_ref, part_ref, s_ref):
     zp, y = lax.axis_index("zp"), lax.axis_index("y")
     q_t = stacked_t(q_ref[...])
     top = jnp.full((8, ROWS), NEGATIVE, jnp.float32)
-    for slot in range(2 * PEERS):
-        peer, part = slot // 2, slot % 2
-        bias = jnp.where(mask[0, window_slot(zp, y, peer, part)] > 0, 0.0, NEGATIVE)
-        raw = jnp.dot(kv_ref[peer, part, 0], q_t, preferred_element_type=jnp.float32) + bias
-        s_ref[slot] = raw
-        top = jnp.maximum(top, raw.reshape(BLK // 8, 8, ROWS).max(axis=0))
+    for first in range(0, 2 * PEERS, FORWARD_STEP):
+        raw = jnp.dot(joined(kv_ref, first, FORWARD_STEP, 0), q_t, preferred_element_type=jnp.float32)
+        for step in range(FORWARD_STEP):
+            slot = first + step
+            bias = jnp.where(mask[0, window_slot(zp, y, slot // 2, slot % 2)] > 0, 0.0, NEGATIVE)
+            block = raw[step * BLK : (step + 1) * BLK] + bias
+            s_ref[slot] = block
+            top = jnp.maximum(top, block.reshape(BLK // 8, 8, ROWS).max(axis=0))
     top = top.max(axis=0, keepdims=True)
     total = jnp.zeros((8, ROWS), jnp.float32)
     numer = jnp.zeros((DH, ROWS), jnp.float32)
-    for slot in range(2 * PEERS):
-        weights = jnp.exp2((s_ref[slot] - top) * EXP2_SCALE)
-        total = total + weights.reshape(BLK // 8, 8, ROWS).sum(axis=0)
-        rounded = weights.astype(jnp.bfloat16)
-        w_ref[slot // 2, slot % 2] = rounded
-        values_t = kv_ref[slot // 2, slot % 2, 1].T
+    for first in range(0, 2 * PEERS, FORWARD_STEP):
+        for slot in range(first, first + FORWARD_STEP):
+            weights = jnp.exp2((s_ref[slot] - top) * EXP2_SCALE)
+            total = total + weights.reshape(BLK // 8, 8, ROWS).sum(axis=0)
+            w_ref[slot] = weights.astype(jnp.bfloat16)
+        rounded = w_ref[first : first + FORWARD_STEP].reshape(FORWARD_STEP * BLK, ROWS)
+        values_t = joined(kv_ref, first, FORWARD_STEP, 1).T
         numer = numer + jnp.dot(values_t, rounded, preferred_element_type=jnp.float32)
     inverse = 1.0 / total.sum(axis=0, keepdims=True)
     attended = numer * inverse
@@ -108,31 +117,34 @@
     do_rows = rows_of(do_t)
     q_rows = stacked(q_ref[...])
     grad = jnp.zeros((DH, ROWS), jnp.float32)
-    for slot in range(2 * PEERS):
-        peer, part = slot // 2, slot % 2
-        weights = w_ref[peer, part]
-        d_prob = jnp.dot(kv_ref[peer, part, 1], do_t, preferred_element_type=jnp.float32)
+    for first in range(0, 2 * PEERS, BACKWARD_STEP):
+        weights = w_ref[first : first + BACKWARD_STEP].reshape(BACKWARD_STEP * BLK, ROWS)
+        d_prob = jnp.dot(joined(kv_ref, first, BACKWARD_STEP, 1), do_t, preferred_element_type=jnp.float32)
         d_score = (weights.astype(jnp.float32) * (d_prob - delta)).astype(jnp.bfloat16)
-        term_k = jnp.dot(d_score, q_rows, preferred_element_type=jnp.float32) * SCALING
-        term_v = jnp.dot(weights, do_rows, preferred_element_type=jnp.float32)
-        terms_ref[peer, part, 0] = term_k.astype(jnp.bfloat16)
-        terms_ref[peer, part, 1] = term_v.astype(jnp.bfloat16)
-        grad = grad + jnp.dot(kv_ref[peer, part, 0].T, d_score, preferred_element_type=jnp.float32)
+        term_k = (jnp.dot(d_score, q_rows, preferred_element_type=jnp.float32) * SCALING).astype(jnp.bfloat16)
+        term_v = jnp.dot(weights, do_rows, preferred_element_type=jnp.float32).astype(jnp.bfloat16)
+        for step in range(BACKWARD_STEP):
+            slot = first + step
+            terms_ref[slot // 2, slot % 2, 0] = term_k[step * BLK : (step + 1) * BLK]
+            terms_ref[slot // 2, slot % 2, 1] = term_v[step * BLK : (step + 1) * BLK]
+        keys_t = joined(kv_ref, first, BACKWARD_STEP, 0).T
+        grad = grad + jnp.dot(keys_t, d_score, preferred_element_type=jnp.float32)
     grad_ref[...] = grad
 
 
-def far_sums_kernel(terms_ref, below_ref, above_ref):
+def far_sums_kernel(terms_ref, first_ref, second_ref):
     zp, y = lax.axis_index("zp"), lax.axis_index("y")
-    below = jnp.zeros((2, BLK, DH), jnp.float32)
-    above = jnp.zeros((2, BLK, DH), jnp.float32)
+    odd = lax.axis_index("zq") % 2
+    first = jnp.zeros((2, BLK, DH), jnp.float32)
+    second = jnp.zeros((2, BLK, DH), jnp.float32)
     for peer in range(PEERS):
-        take = jnp.where(zp == peer // 4, y >= peer % 4, zp == 1)
-        share = jnp.where(take, 1.0, 0.0)
+        below = jnp.where(jnp.where(zp == peer // 4, y >= peer % 4, zp == 1), 1, 0)
+        share = jnp.where(below == odd, 1.0, 0.0)
         term = terms_ref[peer, 1].astype(jnp.float32)
-        below = below + term * share
-        above = above + term * (1.0 - share)
-    below_ref[...] = below.astype(jnp.bfloat16)
-    above_ref[...] = above.astype(jnp.bfloat16)
+        first = first + term * share
+        second = second + term * (1.0 - share)
+    first_ref[...] = first.astype(jnp.bfloat16)
+    second_ref[...] = second.astype(jnp.bfloat16)
 
 
 def near_sums_kernel(terms_ref, grad_ref, normed_ref, gain_ref, sum_ref, grad_out, out_ref):
@@ -144,8 +156,8 @@
     out_ref[...] = (unstacked_t(normed_ref[...]) * gain_ref[...]).astype(jnp.bfloat16)
 
 
-def last_kernel(near_ref, below_ref, above_ref, keys_ref, values_ref):
-    total = near_ref[...] + below_ref[...].astype(jnp.float32) + above_ref[...].astype(jnp.float32)
+def last_kernel(near_ref, first_ref, second_ref, keys_ref, values_ref):
+    total = near_ref[...] + first_ref[...].astype(jnp.float32) + second_ref[...].astype(jnp.float32)
     keys_ref[...] = total[0].astype(jnp.bfloat16)
     values_ref[...] = total[1].astype(jnp.bfloat16)
 
@@ -162,9 +174,12 @@
     return [pl.BlockSpec(memory_space=pltpu.SMEM)] * count
 
 
-def two_planes(array, by):
+def swapped(array, first):
     length = lax.axis_size("zq")
-    return lax.ppermute(array, "zq", [(i, (i + by) % length) for i in range(length)])
+    pairs = []
+    for low in range(0 if first else 1, length - 1, 2):
+        pairs += [(low, low + 1), (low + 1, low)]
+    return lax.ppermute(array, "zq", pairs)
 
 
 def call(kernel, name, outs, smem, vmem, scratch=(), flops=0, size=0):
@@ -191,19 +206,20 @@
 
     first = jnp.arange(2, dtype=jnp.int32)[:, None, None] == 0
     own = jnp.where(first, keys_in[None], values_in[None])
-    above = two_planes(own, -1)
-    below = two_planes(own, 1)
+    got_first = swapped(own, True)
+    got_second = swapped(own, False)
     index = jnp.arange(2 * PEERS, dtype=jnp.int32).reshape(PEERS, 2, 1, 1, 1)
     to_zp, to_y = index // 8, index // 2 % 4
     take_below = jnp.where(to_zp == zp, y >= to_y, zp == 1)
-    chosen = jnp.where(take_below, below[None, None], above[None, None])
+    odd = lax.axis_index("zq") % 2 == 1
+    chosen = jnp.where(take_below == odd, got_first[None, None], got_second[None, None])
     gathered = lax.all_to_all(jnp.where(index % 2 == 0, own[None, None], chosen), PAIR, 0, 0)
 
     scores = [pltpu.VMEM((2 * PEERS, BLK, ROWS), f32)]
     weights, attended, upstream, inverse, part = call(
         forward_kernel,
         "forward",
-        (shape((PEERS, 2, BLK, ROWS), bf16), columns, columns, row, shape((2, BLK), f32)),
+        (shape((2 * PEERS, BLK, ROWS), bf16), columns, columns, row, shape((2, BLK), f32)),
         1, 4, scores, 550_000_000, 5_000_000,
     )(nearby_block_mask, queries, gathered, grad_out, gain)
     sums = lax.all_to_all(jnp.broadcast_to(part[None], (KV_HEADS, 2, BLK)), "head", 0, 0)
@@ -215,16 +231,16 @@
     )(queries, gathered, weights, attended, upstream, inverse, sums)
     returned = lax.all_to_all(terms, PAIR, 0, 0)
     half = shape(block, bf16)
-    to_below, to_above = call(far_sums_kernel, "far_sums", (half, half), 0, 1, (), 1_000_000, 600_000)(returned)
-    from_above = two_planes(to_below, -1)
-    from_below = two_planes(to_above, 1)
+    to_first, to_second = call(far_sums_kernel, "far_sums", (half, half), 0, 1, (), 1_000_000, 600_000)(returned)
+    from_first = swapped(to_first, True)
+    from_second = swapped(to_second, False)
     tall = shape((BLK, GROUP * DH), bf16)
     near_sum, grad_queries, normed_out = call(
         near_sums_kernel, "near_sums", (shape(block, f32), tall, tall), 0, 4, (), 1_000_000, 1_500_000
     )(returned, grad_t, normed_t, gain)
     piece = shape((BLK, DH), bf16)
     grad_keys, grad_values = call(last_kernel, "last", (piece, piece), 0, 3, (), 1_000_000, 300_000)(
-        near_sum, from_below, from_above
+        near_sum, from_first, from_second
     )
     return normed_out, grad_queries, grad_keys, grad_values
 

time: 94.4 us -> 83.8 us (0.89)
  the two profiles are of different devices: /device:TPU:2 before, /device:TPU:64 now
where the time goes in v4:
time: 83.8 us; the launch traced here: 83.5 us
  blocking collectives  44.4 us (53%)
  starting transfers between devices  26.4 us (32%)
  Pallas kernels  6.51 us (8%)
  waiting for transfers between devices  4.23 us (5%)
  other arithmetic  1.19 us (1%)
    ppermute x4, starting transfers between devices, swapped(): return lax.ppermute(array, 'zq', pairs)  26.4 us
    all_to_all x1, blocking collectives, per_device(): returned = lax.all_to_all(terms, PAIR, 0, 0)  18.5 us
    all_to_all x1, blocking collectives, per_device(): lax.all_to_all(jnp.where(index % 2 == 0, own[None, None], chosen), PAIR,...  16.4 us
    all_to_all x1, blocking collectives, per_device(): lax.all_to_all(jnp.broadcast_to(part[None], (KV_HEADS, 2, BLK)), 'head',...  9.49 us
    ppermute x4, waiting for transfers between devices, swapped(): return lax.ppermute(array, 'zq', pairs)  4.23 us
    pallas_call x1, Pallas kernels, per_device(): call(forward_kernel, 'forward', (shape((2 * PEERS, BLK, ROWS), bf16), col...  2.59 us
    pallas_call x1, Pallas kernels, per_device(): call(backward_kernel, 'backward', (shape((PEERS, 2) + block, bf16), colum...  2.18 us
  transfers between devices with their start and end apart: 4, of which 2 were waited for; matrix products, arithmetic and copies ran while one was open for 0% of the time, Pallas kernels for 1%

profile of v4, /device:TPU:64, one launch (start us, length us, event | category | flops | bytes accessed | tf_op | source)
XLA Modules:
  0.0 83.5 jit_solution(2295026574594856570)
XLA Ops:
  0.6 0.0 copy-start.2
  0.6 0.0 copy-start.3
  0.7 0.0 copy-start.1
  0.7 0.0 copy-start
  0.7 1.0 %broadcast_select_fusion = bf16[2,128,128]{2,1,0:T(8,128)(2,1)S(1)} fusion(pred[2]{0:T(512)(128)(4,1)S(1)} %iota_compare_fusion, bf16[128,128]{1,0:T(8,128)(2,1)} %param.8, bf16[128,128]{1,0:T(8,128)(2,1)} %param.7), kind=kLoop, calls=%fused_computation.1 | loop fusion | flops 32768 | bytes 131074 | tf_op jit(solution)/shard_map/jit(_where)/select_n | solution.py:208
  1.6 6.4 %collective-permute-start.1 = (bf16[2,128,128]{2,1,0:T(8,128)(2,1)S(1)}, bf16[2,128,128]{2,1,0:T(8,128)(2,1)S(1)}, u32[]{:S(2)}, u32[]{:S(2)}) collective-permute-start(bf16[2,128,128]{2,1,0:T(8,128)(2,1)S(1)} %broadcast_select_fusion), channel_id=1, source_target_pairs={{64,128},{128,64},{192,256},{256,192},{320,384},{384,320},{448,512... | collective-permute-start | bytes 196616 | tf_op jit(solution)/shard_map/ppermute | solution.py:182
  8.0 8.5 %collective-permute-start = (bf16[2,128,128]{2,1,0:T(8,128)(2,1)S(1)}, bf16[2,128,128]{2,1,0:T(8,128)(2,1)S(1)}, u32[]{:S(2)}, u32[]{:S(2)}) collective-permute-start(bf16[2,128,128]{2,1,0:T(8,128)(2,1)S(1)} %broadcast_select_fusion), channel_id=1, source_target_pairs={{0,64},{64,0},{128,192},{192,128},{256,320},{320,256},{384,448},{4... | collective-permute-start | bytes 196616 | tf_op jit(solution)/shard_map/ppermute | solution.py:182
  16.6 0.0 collective-permute-done.1
  16.6 2.2 %collective-permute-done = bf16[2,128,128]{2,1,0:T(8,128)(2,1)S(1)} collective-permute-done((bf16[2,128,128]{2,1,0:T(8,128)(2,1)S(1)}, bf16[2,128,128]{2,1,0:T(8,128)(2,1)S(1)}, u32[]{:S(2)}, u32[]{:S(2)}) %collective-permute-start) | collective-permute-done | bytes 65568 | tf_op jit(solution)/shard_map/ppermute | solution.py:182
  18.8 0.2 select_select_fusion
  19.0 16.4 %all_to_all.15.kv_ref = bf16[8,2,2,128,128]{4,3,2,1,0:T(8,128)(2,1)S(1)} all-to-all(bf16[8,2,2,128,128]{4,3,2,1,0:T(8,128)(2,1)S(1)} %select_select_fusion), channel_id=1, replica_groups=mesh['zq'=16,'zp'=2,'y'=4,'head'=8] {'zp','y'}, dimensions={0} | all-to-all | bytes 2097152 | tf_op jit(solution)/shard_map/all_to_all | solution.py:216
  35.4 0.0 copy-done.2
  35.4 0.0 copy-done.1
  35.4 2.6 %forward.1 = (bf16[16,128,512]{2,1,0:T(8,128)(2,1)S(1)}, f32[128,512]{1,0:T(8,128)S(1)}, f32[128,512]{1,0:T(8,128)S(1)}, f32[8,512]{1,0:T(8,128)S(1)}, f32[2,128]{1,0:T(2,128)S(1)}) custom-call(s32[1,16]{1,0:T(1,128)S(1)} %copy-done.3, bf16[128,512]{1,0:T(8,128)(2,1)S(1)} %copy-done.2, bf16[8,2,2,128,128]{4,3,2,1,0:T(8,128)(2,1)S(1)} %all_to_all.15.kv_ref, ...), custom_call_target="tpu_custom_call" | custom-call | flops 550000000 | bytes 5000000 | tf_op jit(solution)/shard_map/forward/pallas_call | solution.py:219
  38.0 9.5 %all_to_all.16.sums_ref = f32[8,2,128]{2,1,0:T(2,128)S(1)} all-to-all(f32[8,2,128]{2,1,0:T(2,128)S(1)} %broadcast_in_dim.89), channel_id=1, replica_groups=mesh['zq'=16,'zp'=2,'y'=4,'head'=8] {'head'}, dimensions={0} | all-to-all | bytes 16384 | tf_op jit(solution)/shard_map/all_to_all | solution.py:225
  47.5 2.2 %backward.1 = (bf16[8,2,2,128,128]{4,3,2,1,0:T(8,128)(2,1)S(1)}, f32[128,512]{1,0:T(8,128)S(1)}, f32[128,512]{1,0:T(8,128)S(1)}) custom-call(bf16[128,512]{1,0:T(8,128)(2,1)S(1)} %copy-done.2, bf16[8,2,2,128,128]{4,3,2,1,0:T(8,128)(2,1)S(1)} %all_to_all.15.kv_ref, bf16[16,128,512]{2,1,0:T(8,128)(2,1)S(1)} %get-tuple-element.19.w_ref, ...), custom_call_target="tpu_custom_call" | custom-call | flops 1100000000 | bytes 5000000 | tf_op jit(solution)/shard_map/backward/pallas_call | solution.py:226
  49.7 18.5 %all_to_all.17.terms_ref = bf16[8,2,2,128,128]{4,3,2,1,0:T(8,128)(2,1)S(1)} all-to-all(bf16[8,2,2,128,128]{4,3,2,1,0:T(8,128)(2,1)S(1)} %get-tuple-element.24), channel_id=1, replica_groups=mesh['zq'=16,'zp'=2,'y'=4,'head'=8] {'zp','y'}, dimensions={0} | all-to-all | bytes 2097152 | tf_op jit(solution)/shard_map/all_to_all | solution.py:232
  68.1 0.2 far_sums.1
  68.4 2.0 %collective-permute-start.2 = (bf16[2,128,128]{2,1,0:T(8,128)(2,1)S(1)}, bf16[2,128,128]{2,1,0:T(8,128)(2,1)S(1)}, u32[]{:S(2)}, u32[]{:S(2)}) collective-permute-start(bf16[2,128,128]{2,1,0:T(8,128)(2,1)S(1)} %get-tuple-element.30), channel_id=1, source_target_pairs={{0,64},{64,0},{128,192},{192,128},{256,320},{320,256},{384,448},{4... | collective-permute-start | bytes 196616 | tf_op jit(solution)/shard_map/ppermute | solution.py:182
  70.4 9.6 %collective-permute-start.3 = (bf16[2,128,128]{2,1,0:T(8,128)(2,1)S(1)}, bf16[2,128,128]{2,1,0:T(8,128)(2,1)S(1)}, u32[]{:S(2)}, u32[]{:S(2)}) collective-permute-start(bf16[2,128,128]{2,1,0:T(8,128)(2,1)S(1)} %get-tuple-element.31), channel_id=1, source_target_pairs={{64,128},{128,64},{192,256},{256,192},{320,384},{384,320},{448,512... | collective-permute-start | bytes 196616 | tf_op jit(solution)/shard_map/ppermute | solution.py:182
  80.0 0.9 %near_sums.1 = (f32[2,128,128]{2,1,0:T(8,128)S(1)}, bf16[128,512]{1,0:T(8,128)(2,1)}, bf16[128,512]{1,0:T(8,128)(2,1)}) custom-call(bf16[8,2,2,128,128]{4,3,2,1,0:T(8,128)(2,1)S(1)} %all_to_all.17.terms_ref, f32[128,512]{1,0:T(8,128)S(1)} %get-tuple-element.25.grad_ref, f32[128,512]{1,0:T(8,128)S(1)} %get-tuple-element.26.normed_ref, f32[1,512]{1,0:T(1,128)S(1)} %bitcast.2), custom_call_target="tpu_custom_call" | custom-call | flops 1000000 | bytes 1500000 | tf_op jit(solution)/shard_map/near_sums/pallas_call | solution.py:238
  80.8 0.0 collective-permute-done.2.first_ref
  80.8 2.1 %collective-permute-done.3.second_ref = bf16[2,128,128]{2,1,0:T(8,128)(2,1)S(1)} collective-permute-done((bf16[2,128,128]{2,1,0:T(8,128)(2,1)S(1)}, bf16[2,128,128]{2,1,0:T(8,128)(2,1)S(1)}, u32[]{:S(2)}, u32[]{:S(2)}) %collective-permute-start.3) | collective-permute-done | bytes 65568 | tf_op jit(solution)/shard_map/ppermute | solution.py:182
  82.9 0.6 last.1
  (5 shorter events, 0.0 us)
Async XLA Ops:
  0.6 34.7 %copy-start.2 = (bf16[128,512]{1,0:T(8,128)(2,1)S(1)}, bf16[128,512]{1,0:T(8,128)(2,1)}, u32[]{:S(2)}) copy-start(bf16[128,512]{1,0:T(8,128)(2,1)} %q_ref.3) | copy-start | bytes 393220
  0.6 34.7 %copy-start.3 = (s32[1,16]{1,0:T(1,128)S(1)}, s32[1,16]{1,0:T(1,128)}, u32[]{:S(2)}) copy-start(s32[1,16]{1,0:T(1,128)} %mask.1) | copy-start | bytes 196
  0.7 34.7 %copy-start.1 = (bf16[128,512]{1,0:T(8,128)(2,1)S(1)}, bf16[128,512]{1,0:T(8,128)(2,1)}, u32[]{:S(2)}) copy-start(bf16[128,512]{1,0:T(8,128)(2,1)} %up_ref.1) | copy-start | bytes 393220
  0.7 34.7 %copy-start = (f32[512]{0:T(512)S(1)}, f32[512]{0:T(512)}, u32[]{:S(2)}) copy-start(f32[512]{0:T(512)} %param.9) | copy-start | bytes 6148
  1.6 14.9 %collective-permute-start.1 = (bf16[2,128,128]{2,1,0:T(8,128)(2,1)S(1)}, bf16[2,128,128]{2,1,0:T(8,128)(2,1)S(1)}, u32[]{:S(2)}, u32[]{:S(2)}) collective-permute-start(bf16[2,128,128]{2,1,0:T(8,128)(2,1)S(1)} %broadcast_select_fusion), channel_id=1, source_target_pairs={{64,128},{128,64},{192,256},{256,192},{320,384},{384,320},{448,512... | collective-permute-start | bytes 196616 | tf_op jit(solution)/shard_map/ppermute | solution.py:182
  8.0 10.7 %collective-permute-start = (bf16[2,128,128]{2,1,0:T(8,128)(2,1)S(1)}, bf16[2,128,128]{2,1,0:T(8,128)(2,1)S(1)}, u32[]{:S(2)}, u32[]{:S(2)}) collective-permute-start(bf16[2,128,128]{2,1,0:T(8,128)(2,1)S(1)} %broadcast_select_fusion), channel_id=1, source_target_pairs={{0,64},{64,0},{128,192},{192,128},{256,320},{320,256},{384,448},{4... | collective-permute-start | bytes 196616 | tf_op jit(solution)/shard_map/ppermute | solution.py:182
  68.4 12.5 %collective-permute-start.2 = (bf16[2,128,128]{2,1,0:T(8,128)(2,1)S(1)}, bf16[2,128,128]{2,1,0:T(8,128)(2,1)S(1)}, u32[]{:S(2)}, u32[]{:S(2)}) collective-permute-start(bf16[2,128,128]{2,1,0:T(8,128)(2,1)S(1)} %get-tuple-element.30), channel_id=1, source_target_pairs={{0,64},{64,0},{128,192},{192,128},{256,320},{320,256},{384,448},{4... | collective-permute-start | bytes 196616 | tf_op jit(solution)/shard_map/ppermute | solution.py:182
  70.4 12.5 %collective-permute-start.3 = (bf16[2,128,128]{2,1,0:T(8,128)(2,1)S(1)}, bf16[2,128,128]{2,1,0:T(8,128)(2,1)S(1)}, u32[]{:S(2)}, u32[]{:S(2)}) collective-permute-start(bf16[2,128,128]{2,1,0:T(8,128)(2,1)S(1)} %get-tuple-element.31), channel_id=1, source_target_pairs={{64,128},{128,64},{192,256},{256,192},{320,384},{384,320},{448,512... | collective-permute-start | bytes 196616 | tf_op jit(solution)/shard_map/ppermute | solution.py:182

commit v5 on v4

--- a/solution.py
+++ b/solution.py
@@ -182,6 +182,11 @@
     return lax.ppermute(array, "zq", pairs)
 
 
+def two_planes(array, by):
+    length = lax.axis_size("zq")
+    return lax.ppermute(array, "zq", [(i, i + by) for i in range(length) if 0 <= i + by < length])
+
+
 def call(kernel, name, outs, smem, vmem, scratch=(), flops=0, size=0):
     specs = tuple(in_vmem(len(outs)))
     return pl.pallas_call(
@@ -206,13 +211,12 @@
 
     first = jnp.arange(2, dtype=jnp.int32)[:, None, None] == 0
     own = jnp.where(first, keys_in[None], values_in[None])
-    got_first = swapped(own, True)
-    got_second = swapped(own, False)
+    above = two_planes(own, -1)
+    below = two_planes(own, 1)
     index = jnp.arange(2 * PEERS, dtype=jnp.int32).reshape(PEERS, 2, 1, 1, 1)
     to_zp, to_y = index // 8, index // 2 % 4
     take_below = jnp.where(to_zp == zp, y >= to_y, zp == 1)
-    odd = lax.axis_index("zq") % 2 == 1
-    chosen = jnp.where(take_below == odd, got_first[None, None], got_second[None, None])
+    chosen = jnp.where(take_below, below[None, None], above[None, None])
     gathered = lax.all_to_all(jnp.where(index % 2 == 0, own[None, None], chosen), PAIR, 0, 0)
 
     scores = [pltpu.VMEM((2 * PEERS, BLK, ROWS), f32)]

time: 83.8 us -> 82.2 us (0.981)
  blocking collectives: 44.4 us -> 40 us
  waiting for transfers between devices: 4.23 us -> 7.36 us
    ppermute x4 -> x2, starting transfers between devices: 26.4 us -> 9.98 us  [swapped(): return lax.ppermute(array, 'zq', pairs)]
    ppermute x0 -> x2, starting transfers between devices: none -> 16.1 us  [two_planes(): lax.ppermute(array, 'zq', [(i, i + by) for i in range(length) if 0 <= i +...]
    ppermute x0 -> x2, waiting for transfers between devices: none -> 5.31 us  [two_planes(): lax.ppermute(array, 'zq', [(i, i + by) for i in range(length) if 0 <= i +...]
    all_to_all x1, blocking collectives: 16.4 us -> 13.9 us  [per_device(): lax.all_to_all(jnp.where(index % 2 == 0, own[None, None], chosen), PAIR,...]
    ppermute x4 -> x2, waiting for transfers between devices: 4.23 us -> 2.05 us  [swapped(): return lax.ppermute(array, 'zq', pairs)]
    all_to_all x1, blocking collectives: 9.49 us -> 7.67 us  [per_device(): lax.all_to_all(jnp.broadcast_to(part[None], (KV_HEADS, 2, BLK)), 'head',...]
where the time goes in v5:
time: 82.2 us; the launch traced here: 81.9 us
  blocking collectives  40 us (49%)
  starting transfers between devices  26.1 us (32%)
  waiting for transfers between devices  7.36 us (9%)
  Pallas kernels  6.51 us (8%)
  other arithmetic  1.19 us (1%)
    all_to_all x1, blocking collectives, per_device(): returned = lax.all_to_all(terms, PAIR, 0, 0)  18.5 us
    ppermute x2, starting transfers between devices, two_planes(): lax.ppermute(array, 'zq', [(i, i + by) for i in range(length) if 0 <= i +...  16.1 us
    all_to_all x1, blocking collectives, per_device(): lax.all_to_all(jnp.where(index % 2 == 0, own[None, None], chosen), PAIR,...  13.9 us
    ppermute x2, starting transfers between devices, swapped(): return lax.ppermute(array, 'zq', pairs)  9.98 us
    all_to_all x1, blocking collectives, per_device(): lax.all_to_all(jnp.broadcast_to(part[None], (KV_HEADS, 2, BLK)), 'head',...  7.67 us
    ppermute x2, waiting for transfers between devices, two_planes(): lax.ppermute(array, 'zq', [(i, i + by) for i in range(length) if 0 <= i +...  5.31 us
    pallas_call x1, Pallas kernels, per_device(): call(forward_kernel, 'forward', (shape((2 * PEERS, BLK, ROWS), bf16), col...  2.59 us
    pallas_call x1, Pallas kernels, per_device(): call(backward_kernel, 'backward', (shape((PEERS, 2) + block, bf16), colum...  2.18 us
  transfers between devices with their start and end apart: 4, of which 2 were waited for; matrix products, arithmetic and copies ran while one was open for 0% of the time, Pallas kernels for 1%

profile of v5, /device:TPU:64, one launch (start us, length us, event | category | flops | bytes accessed | tf_op | source)
XLA Modules:
  0.0 81.9 jit_solution(10724215986663649842)
XLA Ops:
  0.6 0.0 copy-start.2
  0.6 0.0 copy-start.3
  0.7 0.0 copy-start.1
  0.7 0.0 copy-start
  0.7 1.0 %broadcast_select_fusion = bf16[2,128,128]{2,1,0:T(8,128)(2,1)S(1)} fusion(pred[2]{0:T(512)(128)(4,1)S(1)} %iota_compare_fusion, bf16[128,128]{1,0:T(8,128)(2,1)} %param.8, bf16[128,128]{1,0:T(8,128)(2,1)} %param.7), kind=kLoop, calls=%fused_computation.1 | loop fusion | flops 32768 | bytes 131074 | tf_op jit(solution)/shard_map/jit(_where)/select_n | solution.py:213
  1.6 14.2 %collective-permute-start.1 = (bf16[2,128,128]{2,1,0:T(8,128)(2,1)S(1)}, bf16[2,128,128]{2,1,0:T(8,128)(2,1)S(1)}, u32[]{:S(2)}, u32[]{:S(2)}) collective-permute-start(bf16[2,128,128]{2,1,0:T(8,128)(2,1)S(1)} %broadcast_select_fusion), channel_id=1, source_target_pairs={{64,0},{128,64},{192,128},{256,192},{320,256},{384,320},{448,384},... | collective-permute-start | bytes 196616 | tf_op jit(solution)/shard_map/ppermute | solution.py:187
  15.8 1.9 %collective-permute-start = (bf16[2,128,128]{2,1,0:T(8,128)(2,1)S(1)}, bf16[2,128,128]{2,1,0:T(8,128)(2,1)S(1)}, u32[]{:S(2)}, u32[]{:S(2)}) collective-permute-start(bf16[2,128,128]{2,1,0:T(8,128)(2,1)S(1)} %broadcast_select_fusion), channel_id=1, source_target_pairs={{0,64},{64,128},{128,192},{192,256},{256,320},{320,384},{384,448},... | collective-permute-start | bytes 196616 | tf_op jit(solution)/shard_map/ppermute | solution.py:187
  17.8 0.0 collective-permute-done.1
  17.8 5.3 %collective-permute-done = bf16[2,128,128]{2,1,0:T(8,128)(2,1)S(1)} collective-permute-done((bf16[2,128,128]{2,1,0:T(8,128)(2,1)S(1)}, bf16[2,128,128]{2,1,0:T(8,128)(2,1)S(1)}, u32[]{:S(2)}, u32[]{:S(2)}) %collective-permute-start) | collective-permute-done | bytes 65568 | tf_op jit(solution)/shard_map/ppermute | solution.py:187
  23.1 0.2 select_select_fusion
  23.3 13.9 %all_to_all.15.kv_ref = bf16[8,2,2,128,128]{4,3,2,1,0:T(8,128)(2,1)S(1)} all-to-all(bf16[8,2,2,128,128]{4,3,2,1,0:T(8,128)(2,1)S(1)} %select_select_fusion), channel_id=1, replica_groups=mesh['zq'=16,'zp'=2,'y'=4,'head'=8] {'zp','y'}, dimensions={0} | all-to-all | bytes 2097152 | tf_op jit(solution)/shard_map/all_to_all | solution.py:220
  37.2 0.0 copy-done.2
  37.2 0.0 copy-done.1
  37.2 2.6 %forward.1 = (bf16[16,128,512]{2,1,0:T(8,128)(2,1)S(1)}, f32[128,512]{1,0:T(8,128)S(1)}, f32[128,512]{1,0:T(8,128)S(1)}, f32[8,512]{1,0:T(8,128)S(1)}, f32[2,128]{1,0:T(2,128)S(1)}) custom-call(s32[1,16]{1,0:T(1,128)S(1)} %copy-done.3, bf16[128,512]{1,0:T(8,128)(2,1)S(1)} %copy-done.2, bf16[8,2,2,128,128]{4,3,2,1,0:T(8,128)(2,1)S(1)} %all_to_all.15.kv_ref, ...), custom_call_target="tpu_custom_call" | custom-call | flops 550000000 | bytes 5000000 | tf_op jit(solution)/shard_map/forward/pallas_call | solution.py:223
  39.8 7.7 %all_to_all.16.sums_ref = f32[8,2,128]{2,1,0:T(2,128)S(1)} all-to-all(f32[8,2,128]{2,1,0:T(2,128)S(1)} %broadcast_in_dim.89), channel_id=1, replica_groups=mesh['zq'=16,'zp'=2,'y'=4,'head'=8] {'head'}, dimensions={0} | all-to-all | bytes 16384 | tf_op jit(solution)/shard_map/all_to_all | solution.py:229
  47.5 2.2 %backward.1 = (bf16[8,2,2,128,128]{4,3,2,1,0:T(8,128)(2,1)S(1)}, f32[128,512]{1,0:T(8,128)S(1)}, f32[128,512]{1,0:T(8,128)S(1)}) custom-call(bf16[128,512]{1,0:T(8,128)(2,1)S(1)} %copy-done.2, bf16[8,2,2,128,128]{4,3,2,1,0:T(8,128)(2,1)S(1)} %all_to_all.15.kv_ref, bf16[16,128,512]{2,1,0:T(8,128)(2,1)S(1)} %get-tuple-element.19.w_ref, ...), custom_call_target="tpu_custom_call" | custom-call | flops 1100000000 | bytes 5000000 | tf_op jit(solution)/shard_map/backward/pallas_call | solution.py:230
  49.7 18.5 %all_to_all.17.terms_ref = bf16[8,2,2,128,128]{4,3,2,1,0:T(8,128)(2,1)S(1)} all-to-all(bf16[8,2,2,128,128]{4,3,2,1,0:T(8,128)(2,1)S(1)} %get-tuple-element.24), channel_id=1, replica_groups=mesh['zq'=16,'zp'=2,'y'=4,'head'=8] {'zp','y'}, dimensions={0} | all-to-all | bytes 2097152 | tf_op jit(solution)/shard_map/all_to_all | solution.py:236
  68.1 0.2 far_sums.1
  68.4 1.9 %collective-permute-start.2 = (bf16[2,128,128]{2,1,0:T(8,128)(2,1)S(1)}, bf16[2,128,128]{2,1,0:T(8,128)(2,1)S(1)}, u32[]{:S(2)}, u32[]{:S(2)}) collective-permute-start(bf16[2,128,128]{2,1,0:T(8,128)(2,1)S(1)} %get-tuple-element.30), channel_id=1, source_target_pairs={{0,64},{64,0},{128,192},{192,128},{256,320},{320,256},{384,448},{4... | collective-permute-start | bytes 196616 | tf_op jit(solution)/shard_map/ppermute | solution.py:182
  70.3 8.1 %collective-permute-start.3 = (bf16[2,128,128]{2,1,0:T(8,128)(2,1)S(1)}, bf16[2,128,128]{2,1,0:T(8,128)(2,1)S(1)}, u32[]{:S(2)}, u32[]{:S(2)}) collective-permute-start(bf16[2,128,128]{2,1,0:T(8,128)(2,1)S(1)} %get-tuple-element.31), channel_id=1, source_target_pairs={{64,128},{128,64},{192,256},{256,192},{320,384},{384,320},{448,512... | collective-permute-start | bytes 196616 | tf_op jit(solution)/shard_map/ppermute | solution.py:182
  78.4 0.9 %near_sums.1 = (f32[2,128,128]{2,1,0:T(8,128)S(1)}, bf16[128,512]{1,0:T(8,128)(2,1)}, bf16[128,512]{1,0:T(8,128)(2,1)}) custom-call(bf16[8,2,2,128,128]{4,3,2,1,0:T(8,128)(2,1)S(1)} %all_to_all.17.terms_ref, f32[128,512]{1,0:T(8,128)S(1)} %get-tuple-element.25.grad_ref, f32[128,512]{1,0:T(8,128)S(1)} %get-tuple-element.26.normed_ref, f32[1,512]{1,0:T(1,128)S(1)} %bitcast.2), custom_call_target="tpu_custom_call" | custom-call | flops 1000000 | bytes 1500000 | tf_op jit(solution)/shard_map/near_sums/pallas_call | solution.py:242
  79.2 0.0 collective-permute-done.2.first_ref
  79.2 2.1 %collective-permute-done.3.second_ref = bf16[2,128,128]{2,1,0:T(8,128)(2,1)S(1)} collective-permute-done((bf16[2,128,128]{2,1,0:T(8,128)(2,1)S(1)}, bf16[2,128,128]{2,1,0:T(8,128)(2,1)S(1)}, u32[]{:S(2)}, u32[]{:S(2)}) %collective-permute-start.3) | collective-permute-done | bytes 65568 | tf_op jit(solution)/shard_map/ppermute | solution.py:182
  81.3 0.6 last.1
  (5 shorter events, 0.0 us)
Async XLA Ops:
  0.6 36.6 %copy-start.2 = (bf16[128,512]{1,0:T(8,128)(2,1)S(1)}, bf16[128,512]{1,0:T(8,128)(2,1)}, u32[]{:S(2)}) copy-start(bf16[128,512]{1,0:T(8,128)(2,1)} %q_ref.3) | copy-start | bytes 393220
  0.6 36.6 %copy-start.3 = (s32[1,16]{1,0:T(1,128)S(1)}, s32[1,16]{1,0:T(1,128)}, u32[]{:S(2)}) copy-start(s32[1,16]{1,0:T(1,128)} %mask.1) | copy-start | bytes 196
  0.7 36.6 %copy-start.1 = (bf16[128,512]{1,0:T(8,128)(2,1)S(1)}, bf16[128,512]{1,0:T(8,128)(2,1)}, u32[]{:S(2)}) copy-start(bf16[128,512]{1,0:T(8,128)(2,1)} %up_ref.1) | copy-start | bytes 393220
  0.7 36.5 %copy-start = (f32[512]{0:T(512)S(1)}, f32[512]{0:T(512)}, u32[]{:S(2)}) copy-start(f32[512]{0:T(512)} %param.9) | copy-start | bytes 6148
  1.6 16.2 %collective-permute-start.1 = (bf16[2,128,128]{2,1,0:T(8,128)(2,1)S(1)}, bf16[2,128,128]{2,1,0:T(8,128)(2,1)S(1)}, u32[]{:S(2)}, u32[]{:S(2)}) collective-permute-start(bf16[2,128,128]{2,1,0:T(8,128)(2,1)S(1)} %broadcast_select_fusion), channel_id=1, source_target_pairs={{64,0},{128,64},{192,128},{256,192},{320,256},{384,320},{448,384},... | collective-permute-start | bytes 196616 | tf_op jit(solution)/shard_map/ppermute | solution.py:187
  15.8 7.3 %collective-permute-start = (bf16[2,128,128]{2,1,0:T(8,128)(2,1)S(1)}, bf16[2,128,128]{2,1,0:T(8,128)(2,1)S(1)}, u32[]{:S(2)}, u32[]{:S(2)}) collective-permute-start(bf16[2,128,128]{2,1,0:T(8,128)(2,1)S(1)} %broadcast_select_fusion), channel_id=1, source_target_pairs={{0,64},{64,128},{128,192},{192,256},{256,320},{320,384},{384,448},... | collective-permute-start | bytes 196616 | tf_op jit(solution)/shard_map/ppermute | solution.py:187
  68.4 10.9 %collective-permute-start.2 = (bf16[2,128,128]{2,1,0:T(8,128)(2,1)S(1)}, bf16[2,128,128]{2,1,0:T(8,128)(2,1)S(1)}, u32[]{:S(2)}, u32[]{:S(2)}) collective-permute-start(bf16[2,128,128]{2,1,0:T(8,128)(2,1)S(1)} %get-tuple-element.30), channel_id=1, source_target_pairs={{0,64},{64,0},{128,192},{192,128},{256,320},{320,256},{384,448},{4... | collective-permute-start | bytes 196616 | tf_op jit(solution)/shard_map/ppermute | solution.py:182
  70.3 11.0 %collective-permute-start.3 = (bf16[2,128,128]{2,1,0:T(8,128)(2,1)S(1)}, bf16[2,128,128]{2,1,0:T(8,128)(2,1)S(1)}, u32[]{:S(2)}, u32[]{:S(2)}) collective-permute-start(bf16[2,128,128]{2,1,0:T(8,128)(2,1)S(1)} %get-tuple-element.31), channel_id=1, source_target_pairs={{64,128},{128,64},{192,256},{256,192},{320,384},{384,320},{448,512... | collective-permute-start | bytes 196616 | tf_op jit(solution)/shard_map/ppermute | solution.py:182

commit v6 on v5

--- a/solution.py
+++ b/solution.py
@@ -132,19 +132,18 @@
     grad_ref[...] = grad
 
 
-def far_sums_kernel(terms_ref, first_ref, second_ref):
+def far_sums_kernel(terms_ref, below_ref, above_ref):
     zp, y = lax.axis_index("zp"), lax.axis_index("y")
-    odd = lax.axis_index("zq") % 2
-    first = jnp.zeros((2, BLK, DH), jnp.float32)
-    second = jnp.zeros((2, BLK, DH), jnp.float32)
+    below = jnp.zeros((2, BLK, DH), jnp.float32)
+    above = jnp.zeros((2, BLK, DH), jnp.float32)
     for peer in range(PEERS):
-        below = jnp.where(jnp.where(zp == peer // 4, y >= peer % 4, zp == 1), 1, 0)
-        share = jnp.where(below == odd, 1.0, 0.0)
+        take = jnp.where(zp == peer // 4, y >= peer % 4, zp == 1)
+        share = jnp.where(take, 1.0, 0.0)
         term = terms_ref[peer, 1].astype(jnp.float32)
-        first = first + term * share
-        second = second + term * (1.0 - share)
-    first_ref[...] = first.astype(jnp.bfloat16)
-    second_ref[...] = second.astype(jnp.bfloat16)
+        below = below + term * share
+        above = above + term * (1.0 - share)
+    below_ref[...] = below.astype(jnp.bfloat16)
+    above_ref[...] = above.astype(jnp.bfloat16)
 
 
 def near_sums_kernel(terms_ref, grad_ref, normed_ref, gain_ref, sum_ref, grad_out, out_ref):
@@ -156,8 +155,8 @@
     out_ref[...] = (unstacked_t(normed_ref[...]) * gain_ref[...]).astype(jnp.bfloat16)
 
 
-def last_kernel(near_ref, first_ref, second_ref, keys_ref, values_ref):
-    total = near_ref[...] + first_ref[...].astype(jnp.float32) + second_ref[...].astype(jnp.float32)
+def last_kernel(near_ref, above_ref, below_ref, keys_ref, values_ref):
+    total = near_ref[...] + below_ref[...].astype(jnp.float32) + above_ref[...].astype(jnp.float32)
     keys_ref[...] = total[0].astype(jnp.bfloat16)
     values_ref[...] = total[1].astype(jnp.bfloat16)
 
@@ -172,14 +171,6 @@
 
 def in_smem(count):
     return [pl.BlockSpec(memory_space=pltpu.SMEM)] * count
-
-
-def swapped(array, first):
-    length = lax.axis_size("zq")
-    pairs = []
-    for low in range(0 if first else 1, length - 1, 2):
-        pairs += [(low, low + 1), (low + 1, low)]
-    return lax.ppermute(array, "zq", pairs)
 
 
 def two_planes(array, by):
@@ -235,16 +226,16 @@
     )(queries, gathered, weights, attended, upstream, inverse, sums)
     returned = lax.all_to_all(terms, PAIR, 0, 0)
     half = shape(block, bf16)
-    to_first, to_second = call(far_sums_kernel, "far_sums", (half, half), 0, 1, (), 1_000_000, 600_000)(returned)
-    from_first = swapped(to_first, True)
-    from_second = swapped(to_second, False)
+    to_below, to_above = call(far_sums_kernel, "far_sums", (half, half), 0, 1, (), 1_000_000, 600_000)(returned)
+    from_above = two_planes(to_below, -1)
+    from_below = two_planes(to_above, 1)
     tall = shape((BLK, GROUP * DH), bf16)
     near_sum, grad_queries, normed_out = call(
         near_sums_kernel, "near_sums", (shape(block, f32), tall, tall), 0, 4, (), 1_000_000, 1_500_000
     )(returned, grad_t, normed_t, gain)
     piece = shape((BLK, DH), bf16)
     grad_keys, grad_values = call(last_kernel, "last", (piece, piece), 0, 3, (), 1_000_000, 300_000)(
-        near_sum, from_first, from_second
+        near_sum, from_above, from_below
     )
     return normed_out, grad_queries, grad_keys, grad_values
 

time: 82.2 us -> 79.2 us (0.964)
  starting transfers between devices: 26.1 us -> 24.1 us
  waiting for transfers between devices: 7.36 us -> 6.31 us
    ppermute x2 -> x0, starting transfers between devices: 9.98 us -> none  [swapped(): return lax.ppermute(array, 'zq', pairs)]
    ppermute x2 -> x4, starting transfers between devices: 16.1 us -> 24.1 us  [two_planes(): lax.ppermute(array, 'zq', [(i, i + by) for i in range(length) if 0 <= i +...]
    ppermute x2 -> x0, waiting for transfers between devices: 2.05 us -> none  [swapped(): return lax.ppermute(array, 'zq', pairs)]
    ppermute x2 -> x4, waiting for transfers between devices: 5.31 us -> 6.31 us  [two_planes(): lax.ppermute(array, 'zq', [(i, i + by) for i in range(length) if 0 <= i +...]
  transfers between devices with their start and end apart: 4 -> 4, of which waited for: 2 -> 3; matrix products, arithmetic and copies ran while one was open for 0% -> 0% of each run, Pallas kernels for 1% -> 1%
where the time goes in v6:
time: 79.2 us; the launch traced here: 78.8 us
  blocking collectives  40 us (51%)
  starting transfers between devices  24.1 us (30%)
  Pallas kernels  6.5 us (8%)
  waiting for transfers between devices  6.31 us (8%)
  other arithmetic  1.19 us (2%)
    ppermute x4, starting transfers between devices, two_planes(): lax.ppermute(array, 'zq', [(i, i + by) for i in range(length) if 0 <= i +...  24.1 us
    all_to_all x1, blocking collectives, per_device(): returned = lax.all_to_all(terms, PAIR, 0, 0)  18.5 us
    all_to_all x1, blocking collectives, per_device(): lax.all_to_all(jnp.where(index % 2 == 0, own[None, None], chosen), PAIR,...  13.9 us
    all_to_all x1, blocking collectives, per_device(): lax.all_to_all(jnp.broadcast_to(part[None], (KV_HEADS, 2, BLK)), 'head',...  7.67 us
    ppermute x4, waiting for transfers between devices, two_planes(): lax.ppermute(array, 'zq', [(i, i + by) for i in range(length) if 0 <= i +...  6.31 us
    pallas_call x1, Pallas kernels, per_device(): call(forward_kernel, 'forward', (shape((2 * PEERS, BLK, ROWS), bf16), col...  2.59 us
    pallas_call x1, Pallas kernels, per_device(): call(backward_kernel, 'backward', (shape((PEERS, 2) + block, bf16), colum...  2.18 us
  transfers between devices with their start and end apart: 4, of which 3 were waited for; matrix products, arithmetic and copies ran while one was open for 0% of the time, Pallas kernels for 1%

profile of v6, /device:TPU:64, one launch (start us, length us, event | category | flops | bytes accessed | tf_op | source)
XLA Modules:
  0.0 78.8 jit_solution(5021253957584536941)
XLA Ops:
  0.6 0.0 copy-start.2
  0.6 0.0 copy-start.3
  0.7 0.0 copy-start.1
  0.7 0.0 copy-start
  0.7 1.0 %broadcast_select_fusion = bf16[2,128,128]{2,1,0:T(8,128)(2,1)S(1)} fusion(pred[2]{0:T(512)(128)(4,1)S(1)} %iota_compare_fusion, bf16[128,128]{1,0:T(8,128)(2,1)} %param.8, bf16[128,128]{1,0:T(8,128)(2,1)} %param.7), kind=kLoop, calls=%fused_computation.1 | loop fusion | flops 32768 | bytes 131074 | tf_op jit(solution)/shard_map/jit(_where)/select_n | solution.py:204
  1.6 14.2 %collective-permute-start.1 = (bf16[2,128,128]{2,1,0:T(8,128)(2,1)S(1)}, bf16[2,128,128]{2,1,0:T(8,128)(2,1)S(1)}, u32[]{:S(2)}, u32[]{:S(2)}) collective-permute-start(bf16[2,128,128]{2,1,0:T(8,128)(2,1)S(1)} %broadcast_select_fusion), channel_id=1, source_target_pairs={{64,0},{128,64},{192,128},{256,192},{320,256},{384,320},{448,384},... | collective-permute-start | bytes 196616 | tf_op jit(solution)/shard_map/ppermute | solution.py:178
  15.8 1.9 %collective-permute-start = (bf16[2,128,128]{2,1,0:T(8,128)(2,1)S(1)}, bf16[2,128,128]{2,1,0:T(8,128)(2,1)S(1)}, u32[]{:S(2)}, u32[]{:S(2)}) collective-permute-start(bf16[2,128,128]{2,1,0:T(8,128)(2,1)S(1)} %broadcast_select_fusion), channel_id=1, source_target_pairs={{0,64},{64,128},{128,192},{192,256},{256,320},{320,384},{384,448},... | collective-permute-start | bytes 196616 | tf_op jit(solution)/shard_map/ppermute | solution.py:178
  17.8 0.0 collective-permute-done.1
  17.8 5.3 %collective-permute-done = bf16[2,128,128]{2,1,0:T(8,128)(2,1)S(1)} collective-permute-done((bf16[2,128,128]{2,1,0:T(8,128)(2,1)S(1)}, bf16[2,128,128]{2,1,0:T(8,128)(2,1)S(1)}, u32[]{:S(2)}, u32[]{:S(2)}) %collective-permute-start) | collective-permute-done | bytes 65568 | tf_op jit(solution)/shard_map/ppermute | solution.py:178
  23.1 0.2 select_select_fusion
  23.3 13.9 %all_to_all.15.kv_ref = bf16[8,2,2,128,128]{4,3,2,1,0:T(8,128)(2,1)S(1)} all-to-all(bf16[8,2,2,128,128]{4,3,2,1,0:T(8,128)(2,1)S(1)} %select_select_fusion), channel_id=1, replica_groups=mesh['zq'=16,'zp'=2,'y'=4,'head'=8] {'zp','y'}, dimensions={0} | all-to-all | bytes 2097152 | tf_op jit(solution)/shard_map/all_to_all | solution.py:211
  37.2 0.0 copy-done.2
  37.2 0.0 copy-done.1
  37.2 2.6 %forward.1 = (bf16[16,128,512]{2,1,0:T(8,128)(2,1)S(1)}, f32[128,512]{1,0:T(8,128)S(1)}, f32[128,512]{1,0:T(8,128)S(1)}, f32[8,512]{1,0:T(8,128)S(1)}, f32[2,128]{1,0:T(2,128)S(1)}) custom-call(s32[1,16]{1,0:T(1,128)S(1)} %copy-done.3, bf16[128,512]{1,0:T(8,128)(2,1)S(1)} %copy-done.2, bf16[8,2,2,128,128]{4,3,2,1,0:T(8,128)(2,1)S(1)} %all_to_all.15.kv_ref, ...), custom_call_target="tpu_custom_call" | custom-call | flops 550000000 | bytes 5000000 | tf_op jit(solution)/shard_map/forward/pallas_call | solution.py:214
  39.8 7.7 %all_to_all.16.sums_ref = f32[8,2,128]{2,1,0:T(2,128)S(1)} all-to-all(f32[8,2,128]{2,1,0:T(2,128)S(1)} %broadcast_in_dim.89), channel_id=1, replica_groups=mesh['zq'=16,'zp'=2,'y'=4,'head'=8] {'head'}, dimensions={0} | all-to-all | bytes 16384 | tf_op jit(solution)/shard_map/all_to_all | solution.py:220
  47.5 2.2 %backward.1 = (bf16[8,2,2,128,128]{4,3,2,1,0:T(8,128)(2,1)S(1)}, f32[128,512]{1,0:T(8,128)S(1)}, f32[128,512]{1,0:T(8,128)S(1)}) custom-call(bf16[128,512]{1,0:T(8,128)(2,1)S(1)} %copy-done.2, bf16[8,2,2,128,128]{4,3,2,1,0:T(8,128)(2,1)S(1)} %all_to_all.15.kv_ref, bf16[16,128,512]{2,1,0:T(8,128)(2,1)S(1)} %get-tuple-element.19.w_ref, ...), custom_call_target="tpu_custom_call" | custom-call | flops 1100000000 | bytes 5000000 | tf_op jit(solution)/shard_map/backward/pallas_call | solution.py:221
  49.7 18.5 %all_to_all.17.terms_ref = bf16[8,2,2,128,128]{4,3,2,1,0:T(8,128)(2,1)S(1)} all-to-all(bf16[8,2,2,128,128]{4,3,2,1,0:T(8,128)(2,1)S(1)} %get-tuple-element.24), channel_id=1, replica_groups=mesh['zq'=16,'zp'=2,'y'=4,'head'=8] {'zp','y'}, dimensions={0} | all-to-all | bytes 2097152 | tf_op jit(solution)/shard_map/all_to_all | solution.py:227
  68.1 0.2 far_sums.1
  68.4 1.9 %collective-permute-start.2 = (bf16[2,128,128]{2,1,0:T(8,128)(2,1)S(1)}, bf16[2,128,128]{2,1,0:T(8,128)(2,1)S(1)}, u32[]{:S(2)}, u32[]{:S(2)}) collective-permute-start(bf16[2,128,128]{2,1,0:T(8,128)(2,1)S(1)} %get-tuple-element.30), channel_id=1, source_target_pairs={{64,0},{128,64},{192,128},{256,192},{320,256},{384,320},{448,384},... | collective-permute-start | bytes 196616 | tf_op jit(solution)/shard_map/ppermute | solution.py:178
  70.3 6.0 %collective-permute-start.3 = (bf16[2,128,128]{2,1,0:T(8,128)(2,1)S(1)}, bf16[2,128,128]{2,1,0:T(8,128)(2,1)S(1)}, u32[]{:S(2)}, u32[]{:S(2)}) collective-permute-start(bf16[2,128,128]{2,1,0:T(8,128)(2,1)S(1)} %get-tuple-element.31), channel_id=1, source_target_pairs={{0,64},{64,128},{128,192},{192,256},{256,320},{320,384},{384,448},... | collective-permute-start | bytes 196616 | tf_op jit(solution)/shard_map/ppermute | solution.py:178
  76.3 0.9 %near_sums.1 = (f32[2,128,128]{2,1,0:T(8,128)S(1)}, bf16[128,512]{1,0:T(8,128)(2,1)}, bf16[128,512]{1,0:T(8,128)(2,1)}) custom-call(bf16[8,2,2,128,128]{4,3,2,1,0:T(8,128)(2,1)S(1)} %all_to_all.17.terms_ref, f32[128,512]{1,0:T(8,128)S(1)} %get-tuple-element.25.grad_ref, f32[128,512]{1,0:T(8,128)S(1)} %get-tuple-element.26.normed_ref, f32[1,512]{1,0:T(1,128)S(1)} %bitcast.2), custom_call_target="tpu_custom_call" | custom-call | flops 1000000 | bytes 1500000 | tf_op jit(solution)/shard_map/near_sums/pallas_call | solution.py:233
  77.2 0.1 collective-permute-done.2.above_ref
  77.3 0.9 %collective-permute-done.3.below_ref = bf16[2,128,128]{2,1,0:T(8,128)(2,1)S(1)} collective-permute-done((bf16[2,128,128]{2,1,0:T(8,128)(2,1)S(1)}, bf16[2,128,128]{2,1,0:T(8,128)(2,1)S(1)}, u32[]{:S(2)}, u32[]{:S(2)}) %collective-permute-start.3) | collective-permute-done | bytes 65568 | tf_op jit(solution)/shard_map/ppermute | solution.py:178
  78.2 0.6 last.1
  (5 shorter events, 0.0 us)
Async XLA Ops:
  0.6 36.6 %copy-start.2 = (bf16[128,512]{1,0:T(8,128)(2,1)S(1)}, bf16[128,512]{1,0:T(8,128)(2,1)}, u32[]{:S(2)}) copy-start(bf16[128,512]{1,0:T(8,128)(2,1)} %q_ref.3) | copy-start | bytes 393220
  0.6 36.6 %copy-start.3 = (s32[1,16]{1,0:T(1,128)S(1)}, s32[1,16]{1,0:T(1,128)}, u32[]{:S(2)}) copy-start(s32[1,16]{1,0:T(1,128)} %mask.1) | copy-start | bytes 196
  0.7 36.6 %copy-start.1 = (bf16[128,512]{1,0:T(8,128)(2,1)S(1)}, bf16[128,512]{1,0:T(8,128)(2,1)}, u32[]{:S(2)}) copy-start(bf16[128,512]{1,0:T(8,128)(2,1)} %up_ref.1) | copy-start | bytes 393220
  0.7 36.5 %copy-start = (f32[512]{0:T(512)S(1)}, f32[512]{0:T(512)}, u32[]{:S(2)}) copy-start(f32[512]{0:T(512)} %param.9) | copy-start | bytes 6148
  1.6 16.2 %collective-permute-start.1 = (bf16[2,128,128]{2,1,0:T(8,128)(2,1)S(1)}, bf16[2,128,128]{2,1,0:T(8,128)(2,1)S(1)}, u32[]{:S(2)}, u32[]{:S(2)}) collective-permute-start(bf16[2,128,128]{2,1,0:T(8,128)(2,1)S(1)} %broadcast_select_fusion), channel_id=1, source_target_pairs={{64,0},{128,64},{192,128},{256,192},{320,256},{384,320},{448,384},... | collective-permute-start | bytes 196616 | tf_op jit(solution)/shard_map/ppermute | solution.py:178
  15.8 7.3 %collective-permute-start = (bf16[2,128,128]{2,1,0:T(8,128)(2,1)S(1)}, bf16[2,128,128]{2,1,0:T(8,128)(2,1)S(1)}, u32[]{:S(2)}, u32[]{:S(2)}) collective-permute-start(bf16[2,128,128]{2,1,0:T(8,128)(2,1)S(1)} %broadcast_select_fusion), channel_id=1, source_target_pairs={{0,64},{64,128},{128,192},{192,256},{256,320},{320,384},{384,448},... | collective-permute-start | bytes 196616 | tf_op jit(solution)/shard_map/ppermute | solution.py:178
  68.4 9.0 %collective-permute-start.2 = (bf16[2,128,128]{2,1,0:T(8,128)(2,1)S(1)}, bf16[2,128,128]{2,1,0:T(8,128)(2,1)S(1)}, u32[]{:S(2)}, u32[]{:S(2)}) collective-permute-start(bf16[2,128,128]{2,1,0:T(8,128)(2,1)S(1)} %get-tuple-element.30), channel_id=1, source_target_pairs={{64,0},{128,64},{192,128},{256,192},{320,256},{384,320},{448,384},... | collective-permute-start | bytes 196616 | tf_op jit(solution)/shard_map/ppermute | solution.py:178
  70.3 7.9 %collective-permute-start.3 = (bf16[2,128,128]{2,1,0:T(8,128)(2,1)S(1)}, bf16[2,128,128]{2,1,0:T(8,128)(2,1)S(1)}, u32[]{:S(2)}, u32[]{:S(2)}) collective-permute-start(bf16[2,128,128]{2,1,0:T(8,128)(2,1)S(1)} %get-tuple-element.31), channel_id=1, source_target_pairs={{0,64},{64,128},{128,192},{192,256},{256,320},{320,384},{384,448},... | collective-permute-start | bytes 196616 | tf_op jit(solution)/shard_map/ppermute | solution.py:178

commit v7 on v6

--- a/solution.py
+++ b/solution.py
@@ -200,8 +200,7 @@
     columns = shape((DH, ROWS), f32)
     row = shape((8, ROWS), f32)
 
-    first = jnp.arange(2, dtype=jnp.int32)[:, None, None] == 0
-    own = jnp.where(first, keys_in[None], values_in[None])
+    own = jnp.stack([keys_in, values_in])
     above = two_planes(own, -1)
     below = two_planes(own, 1)
     index = jnp.arange(2 * PEERS, dtype=jnp.int32).reshape(PEERS, 2, 1, 1, 1)

time: 79.2 us -> 79.1 us (level)
  the two profiles are of different devices: /device:TPU:64 before, /device:TPU:704 now
where the time goes in v7:
time: 79.1 us; the launch traced here: 78.8 us
  blocking collectives  47.6 us (60%)
  starting transfers between devices  15.9 us (20%)
  waiting for transfers between devices  6.96 us (9%)
  Pallas kernels  6.5 us (8%)
  other arithmetic  1.08 us (1%)
    all_to_all x1, blocking collectives, per_device(): lax.all_to_all(jnp.where(index % 2 == 0, own[None, None], chosen), PAIR,...  19.8 us
    all_to_all x1, blocking collectives, per_device(): returned = lax.all_to_all(terms, PAIR, 0, 0)  18.5 us
    ppermute x4, starting transfers between devices, two_planes(): lax.ppermute(array, 'zq', [(i, i + by) for i in range(length) if 0 <= i +...  15.9 us
    all_to_all x1, blocking collectives, per_device(): lax.all_to_all(jnp.broadcast_to(part[None], (KV_HEADS, 2, BLK)), 'head',...  9.41 us
    ppermute x4, waiting for transfers between devices, two_planes(): lax.ppermute(array, 'zq', [(i, i + by) for i in range(length) if 0 <= i +...  6.96 us
    pallas_call x1, Pallas kernels, per_device(): call(forward_kernel, 'forward', (shape((2 * PEERS, BLK, ROWS), bf16), col...  2.59 us
    pallas_call x1, Pallas kernels, per_device(): call(backward_kernel, 'backward', (shape((PEERS, 2) + block, bf16), colum...  2.18 us
  transfers between devices with their start and end apart: 4, of which 4 were waited for; matrix products, arithmetic and copies ran while one was open for 0% of the time, Pallas kernels for 1%

profile of v7, /device:TPU:704, one launch (start us, length us, event | category | flops | bytes accessed | tf_op | source)
XLA Modules:
  0.0 78.8 jit_solution(525591280533382104)
XLA Ops:
  0.6 0.0 copy-start.2
  0.6 0.0 copy-start.3
  0.7 0.0 copy-start.1
  0.7 0.0 copy-start
  0.7 0.9 %pad_maximum_fusion = bf16[2,128,128]{2,1,0:T(8,128)(2,1)S(1)} fusion(bf16[1,128,128]{2,1,0:T(8,128)(2,1)} %bitcast.5, bf16[1,128,128]{2,1,0:T(8,128)(2,1)} %bitcast.6), kind=kLoop, calls=%fused_computation.1 | loop fusion | flops 32768 | bytes 131072 | tf_op jit(solution)/shard_map/stack | solution.py:203
  1.5 3.3 %collective-permute-start.1 = (bf16[2,128,128]{2,1,0:T(8,128)(2,1)S(1)}, bf16[2,128,128]{2,1,0:T(8,128)(2,1)S(1)}, u32[]{:S(2)}, u32[]{:S(2)}) collective-permute-start(bf16[2,128,128]{2,1,0:T(8,128)(2,1)S(1)} %pad_maximum_fusion), channel_id=1, source_target_pairs={{64,0},{128,64},{192,128},{256,192},{320,256},{384,320},{448,384},... | collective-permute-start | bytes 196616 | tf_op jit(solution)/shard_map/ppermute | solution.py:178
  4.9 4.6 %collective-permute-start = (bf16[2,128,128]{2,1,0:T(8,128)(2,1)S(1)}, bf16[2,128,128]{2,1,0:T(8,128)(2,1)S(1)}, u32[]{:S(2)}, u32[]{:S(2)}) collective-permute-start(bf16[2,128,128]{2,1,0:T(8,128)(2,1)S(1)} %pad_maximum_fusion), channel_id=1, source_target_pairs={{0,64},{64,128},{128,192},{192,256},{256,320},{320,384},{384,448},... | collective-permute-start | bytes 196616 | tf_op jit(solution)/shard_map/ppermute | solution.py:178
  9.5 0.9 %collective-permute-done.1 = bf16[2,128,128]{2,1,0:T(8,128)(2,1)S(1)} collective-permute-done((bf16[2,128,128]{2,1,0:T(8,128)(2,1)S(1)}, bf16[2,128,128]{2,1,0:T(8,128)(2,1)S(1)}, u32[]{:S(2)}, u32[]{:S(2)}) %collective-permute-start.1) | collective-permute-done | bytes 65568 | tf_op jit(solution)/shard_map/ppermute | solution.py:178
  10.4 1.7 %collective-permute-done = bf16[2,128,128]{2,1,0:T(8,128)(2,1)S(1)} collective-permute-done((bf16[2,128,128]{2,1,0:T(8,128)(2,1)S(1)}, bf16[2,128,128]{2,1,0:T(8,128)(2,1)S(1)}, u32[]{:S(2)}, u32[]{:S(2)}) %collective-permute-start) | collective-permute-done | bytes 65568 | tf_op jit(solution)/shard_map/ppermute | solution.py:178
  12.0 0.2 select_select_fusion
  12.3 19.8 %all_to_all.15.kv_ref = bf16[8,2,2,128,128]{4,3,2,1,0:T(8,128)(2,1)S(1)} all-to-all(bf16[8,2,2,128,128]{4,3,2,1,0:T(8,128)(2,1)S(1)} %select_select_fusion), channel_id=1, replica_groups=mesh['zq'=16,'zp'=2,'y'=4,'head'=8] {'zp','y'}, dimensions={0} | all-to-all | bytes 2097152 | tf_op jit(solution)/shard_map/all_to_all | solution.py:210
  32.0 0.0 copy-done.2
  32.0 0.0 copy-done.1
  32.0 2.6 %forward.1 = (bf16[16,128,512]{2,1,0:T(8,128)(2,1)S(1)}, f32[128,512]{1,0:T(8,128)S(1)}, f32[128,512]{1,0:T(8,128)S(1)}, f32[8,512]{1,0:T(8,128)S(1)}, f32[2,128]{1,0:T(2,128)S(1)}) custom-call(s32[1,16]{1,0:T(1,128)S(1)} %copy-done.3, bf16[128,512]{1,0:T(8,128)(2,1)S(1)} %copy-done.2, bf16[8,2,2,128,128]{4,3,2,1,0:T(8,128)(2,1)S(1)} %all_to_all.15.kv_ref, ...), custom_call_target="tpu_custom_call" | custom-call | flops 550000000 | bytes 5000000 | tf_op jit(solution)/shard_map/forward/pallas_call | solution.py:213
  34.6 9.4 %all_to_all.16.sums_ref = f32[8,2,128]{2,1,0:T(2,128)S(1)} all-to-all(f32[8,2,128]{2,1,0:T(2,128)S(1)} %broadcast_in_dim.59), channel_id=1, replica_groups=mesh['zq'=16,'zp'=2,'y'=4,'head'=8] {'head'}, dimensions={0} | all-to-all | bytes 16384 | tf_op jit(solution)/shard_map/all_to_all | solution.py:219
  44.0 2.2 %backward.1 = (bf16[8,2,2,128,128]{4,3,2,1,0:T(8,128)(2,1)S(1)}, f32[128,512]{1,0:T(8,128)S(1)}, f32[128,512]{1,0:T(8,128)S(1)}) custom-call(bf16[128,512]{1,0:T(8,128)(2,1)S(1)} %copy-done.2, bf16[8,2,2,128,128]{4,3,2,1,0:T(8,128)(2,1)S(1)} %all_to_all.15.kv_ref, bf16[16,128,512]{2,1,0:T(8,128)(2,1)S(1)} %get-tuple-element.19.w_ref, ...), custom_call_target="tpu_custom_call" | custom-call | flops 1100000000 | bytes 5000000 | tf_op jit(solution)/shard_map/backward/pallas_call | solution.py:220
  46.2 18.5 %all_to_all.17.terms_ref = bf16[8,2,2,128,128]{4,3,2,1,0:T(8,128)(2,1)S(1)} all-to-all(bf16[8,2,2,128,128]{4,3,2,1,0:T(8,128)(2,1)S(1)} %get-tuple-element.24), channel_id=1, replica_groups=mesh['zq'=16,'zp'=2,'y'=4,'head'=8] {'zp','y'}, dimensions={0} | all-to-all | bytes 2097152 | tf_op jit(solution)/shard_map/all_to_all | solution.py:226
  64.7 0.2 far_sums.1
  64.9 5.5 %collective-permute-start.2 = (bf16[2,128,128]{2,1,0:T(8,128)(2,1)S(1)}, bf16[2,128,128]{2,1,0:T(8,128)(2,1)S(1)}, u32[]{:S(2)}, u32[]{:S(2)}) collective-permute-start(bf16[2,128,128]{2,1,0:T(8,128)(2,1)S(1)} %get-tuple-element.30), channel_id=1, source_target_pairs={{64,0},{128,64},{192,128},{256,192},{320,256},{384,320},{448,384},... | collective-permute-start | bytes 196616 | tf_op jit(solution)/shard_map/ppermute | solution.py:178
  70.4 2.4 %collective-permute-start.3 = (bf16[2,128,128]{2,1,0:T(8,128)(2,1)S(1)}, bf16[2,128,128]{2,1,0:T(8,128)(2,1)S(1)}, u32[]{:S(2)}, u32[]{:S(2)}) collective-permute-start(bf16[2,128,128]{2,1,0:T(8,128)(2,1)S(1)} %get-tuple-element.31), channel_id=1, source_target_pairs={{0,64},{64,128},{128,192},{192,256},{256,320},{320,384},{384,448},... | collective-permute-start | bytes 196616 | tf_op jit(solution)/shard_map/ppermute | solution.py:178
  72.9 0.9 %near_sums.1 = (f32[2,128,128]{2,1,0:T(8,128)S(1)}, bf16[128,512]{1,0:T(8,128)(2,1)}, bf16[128,512]{1,0:T(8,128)(2,1)}) custom-call(bf16[8,2,2,128,128]{4,3,2,1,0:T(8,128)(2,1)S(1)} %all_to_all.17.terms_ref, f32[128,512]{1,0:T(8,128)S(1)} %get-tuple-element.25.grad_ref, f32[128,512]{1,0:T(8,128)S(1)} %get-tuple-element.26.normed_ref, f32[1,512]{1,0:T(1,128)S(1)} %bitcast.4), custom_call_target="tpu_custom_call" | custom-call | flops 1000000 | bytes 1500000 | tf_op jit(solution)/shard_map/near_sums/pallas_call | solution.py:232
  73.7 0.1 collective-permute-done.2.above_ref
  73.9 4.3 %collective-permute-done.3.below_ref = bf16[2,128,128]{2,1,0:T(8,128)(2,1)S(1)} collective-permute-done((bf16[2,128,128]{2,1,0:T(8,128)(2,1)S(1)}, bf16[2,128,128]{2,1,0:T(8,128)(2,1)S(1)}, u32[]{:S(2)}, u32[]{:S(2)}) %collective-permute-start.3) | collective-permute-done | bytes 65568 | tf_op jit(solution)/shard_map/ppermute | solution.py:178
  78.2 0.6 last.1
  (4 shorter events, 0.0 us)
Async XLA Ops:
  0.6 31.4 %copy-start.2 = (bf16[128,512]{1,0:T(8,128)(2,1)S(1)}, bf16[128,512]{1,0:T(8,128)(2,1)}, u32[]{:S(2)}) copy-start(bf16[128,512]{1,0:T(8,128)(2,1)} %q_ref.3) | copy-start | bytes 393220
  0.6 31.4 %copy-start.3 = (s32[1,16]{1,0:T(1,128)S(1)}, s32[1,16]{1,0:T(1,128)}, u32[]{:S(2)}) copy-start(s32[1,16]{1,0:T(1,128)} %mask.1) | copy-start | bytes 196
  0.7 31.4 %copy-start.1 = (bf16[128,512]{1,0:T(8,128)(2,1)S(1)}, bf16[128,512]{1,0:T(8,128)(2,1)}, u32[]{:S(2)}) copy-start(bf16[128,512]{1,0:T(8,128)(2,1)} %up_ref.1) | copy-start | bytes 393220
  0.7 31.4 %copy-start = (f32[512]{0:T(512)S(1)}, f32[512]{0:T(512)}, u32[]{:S(2)}) copy-start(f32[512]{0:T(512)} %param.9) | copy-start | bytes 6148
  1.5 8.9 %collective-permute-start.1 = (bf16[2,128,128]{2,1,0:T(8,128)(2,1)S(1)}, bf16[2,128,128]{2,1,0:T(8,128)(2,1)S(1)}, u32[]{:S(2)}, u32[]{:S(2)}) collective-permute-start(bf16[2,128,128]{2,1,0:T(8,128)(2,1)S(1)} %pad_maximum_fusion), channel_id=1, source_target_pairs={{64,0},{128,64},{192,128},{256,192},{320,256},{384,320},{448,384},... | collective-permute-start | bytes 196616 | tf_op jit(solution)/shard_map/ppermute | solution.py:178
  4.9 7.2 %collective-permute-start = (bf16[2,128,128]{2,1,0:T(8,128)(2,1)S(1)}, bf16[2,128,128]{2,1,0:T(8,128)(2,1)S(1)}, u32[]{:S(2)}, u32[]{:S(2)}) collective-permute-start(bf16[2,128,128]{2,1,0:T(8,128)(2,1)S(1)} %pad_maximum_fusion), channel_id=1, source_target_pairs={{0,64},{64,128},{128,192},{192,256},{256,320},{320,384},{384,448},... | collective-permute-start | bytes 196616 | tf_op jit(solution)/shard_map/ppermute | solution.py:178
  64.9 9.0 %collective-permute-start.2 = (bf16[2,128,128]{2,1,0:T(8,128)(2,1)S(1)}, bf16[2,128,128]{2,1,0:T(8,128)(2,1)S(1)}, u32[]{:S(2)}, u32[]{:S(2)}) collective-permute-start(bf16[2,128,128]{2,1,0:T(8,128)(2,1)S(1)} %get-tuple-element.30), channel_id=1, source_target_pairs={{64,0},{128,64},{192,128},{256,192},{320,256},{384,320},{448,384},... | collective-permute-start | bytes 196616 | tf_op jit(solution)/shard_map/ppermute | solution.py:178
  70.4 7.8 %collective-permute-start.3 = (bf16[2,128,128]{2,1,0:T(8,128)(2,1)S(1)}, bf16[2,128,128]{2,1,0:T(8,128)(2,1)S(1)}, u32[]{:S(2)}, u32[]{:S(2)}) collective-permute-start(bf16[2,128,128]{2,1,0:T(8,128)(2,1)S(1)} %get-tuple-element.31), channel_id=1, source_target_pairs={{0,64},{64,128},{128,192},{192,256},{256,320},{320,384},{384,448},... | collective-permute-start | bytes 196616 | tf_op jit(solution)/shard_map/ppermute | solution.py:178
